TPU v7x, 512 devices: a whole 4x4x16 slice. The times are simulated.
512 devices in a mesh: group: 16 (over x, z_lo), dp: 32 (over y, z_hi, core).
Axes of the slice: x: 4, y: 4, z: 16 (z_hi: 4, z_lo: 4; z = z_hi * 4 + z_lo), core: 2. Of those that a mesh axis runs over, the one named last changes fastest.
Arguments:
- embeddings: float32 [131072, 512], P(('group', 'dp')), may hold values from -8 to 8
- partner: int32 [131072], replicated, may hold values from 0 to 131071, as said below
Outputs:
- gradient: float32 [131072, 512], P(('group', 'dp'))
- loss: float32 [], replicated
Inputs may be any that keep to these rules, and one draw needn't show every extreme that they name: partner[partner[i]] == i and partner[i] != i, and partner[i] lies in the same batch as i: the rows of each batch form 4096/2 pairs of views, drawn at random.
All inputs are finite; a program needn't handle non-finite values.
Results may differ from a plain program's by a relative error of at most 0.00095.
The roundings to bfloat16 on the way count: a program that leaves them out, or rounds other values in their place, can miss the bound.
Values may be sent and summed in bfloat16 or wider, within the bound.
No kernel may reach another device: no remote copies, remote signals or barrier semaphores. Data moves between devices by JAX's collectives and lax.ppermute only.
A program may use at most 64 MiB of HBM per device.

v0:
```python
import jax
import jax.numpy as jnp
from jax import lax
from jax.sharding import PartitionSpec as P

TAU = 0.1


def tile_expo(own_units, col_units, own_index, col_index):
    scores = jnp.dot(own_units, col_units.T, preferred_element_type=jnp.float32) / TAU
    on_diagonal = own_index[:, None] == col_index[None, :]
    weights_exp = jnp.where(on_diagonal, jnp.float32(0.0), jnp.exp(scores - 1.0 / TAU))
    return (scores, weights_exp)


def tile_grad(weights_exp, is_partner, own_totals, col_totals, col_units):
    indicator = is_partner.astype(jnp.float32)
    row_weights = (weights_exp / own_totals[:, None] - indicator).astype(jnp.bfloat16)
    col_weights = (weights_exp / col_totals[None, :] - indicator).astype(jnp.bfloat16)
    both = jnp.concatenate([row_weights, col_weights], axis=0)
    summed = jnp.dot(both, col_units, preferred_element_type=jnp.float32)
    half = row_weights.shape[0]
    return summed[:half] + summed[half:]


def share_totals(own_totals):
    return lax.all_gather(own_totals, "group", axis=0, tiled=True)


def on_device(embeddings, partner):
    rows_local = embeddings.shape[0]
    inner_count = lax.axis_size("dp")
    outer_count = lax.axis_size("group")
    inner_pos = lax.axis_index("dp")
    outer_pos = lax.axis_index("group")
    lengths = jnp.sqrt(jnp.sum(embeddings * embeddings, axis=1, keepdims=True) + 1e-06)
    unit = embeddings / lengths
    packed = unit.astype(jnp.bfloat16)
    span = rows_local * outer_count
    own_index = outer_pos * rows_local + jnp.arange(rows_local, dtype=jnp.int32)
    global_start = (outer_pos * inner_count + inner_pos) * rows_local
    partner_global = lax.dynamic_slice_in_dim(partner, global_start, rows_local, 0)
    partner_local = (
        partner_global // (inner_count * rows_local) * rows_local + partner_global % rows_local
    )
    batch_units = lax.all_gather(packed, "group", axis=0, tiled=True)
    col_index = jnp.arange(span, dtype=jnp.int32)
    scores, weights_exp = tile_expo(packed, batch_units, own_index, col_index)
    is_partner = col_index[None, :] == partner_local[:, None]
    own_totals = jnp.sum(weights_exp, axis=1)
    positive = jnp.sum(jnp.where(is_partner, scores, jnp.float32(0.0)), axis=1)
    all_totals = share_totals(own_totals)
    own_grad = tile_grad(weights_exp, is_partner, own_totals, all_totals, batch_units)
    loss_rows = jnp.log(own_totals) + 1.0 / TAU - positive
    loss_total = lax.psum(jnp.sum(loss_rows), ("group", "dp"))
    unit_grad = own_grad / TAU
    gradient = (unit_grad - unit * jnp.sum(unit * unit_grad, axis=1, keepdims=True)) / lengths
    loss = loss_total / (rows_local * inner_count * outer_count)
    return (gradient, loss)


def solution(mesh):
    placed = (P(("group", "dp"), None), P())
    return jax.shard_map(
        on_device,
        mesh=mesh,
        in_specs=placed,
        out_specs=(P(("group", "dp"), None), P()),
        check_vma=False,
    )
```

profile of v0, /device:TPU:1, one launch (start us, length us, event | category | flops | bytes accessed | tf_op | source)
XLA Modules:
  0.0 293.7 jit_solution(8131938232122846551)
XLA Ops:
  7.2 0.0 all-gather.3.cloned.1.call-start
  7.2 1.2 multiply_reduce_fusion.1
  8.4 1.2 copy.6
  9.6 0.7 fusion.10
  10.4 0.0 all-gather.3.cloned.1.call-update
  10.4 0.8 fusion.8
  11.2 115.8 %all-gather.3.cloned.1.call-done = bf16[4096,512]{0,1:T(8,128)(2,1)} async-done(((bf16[256,512]{0,1:T(8,128)(2,1)}), bf16[4096,512]{0,1:T(8,128)(2,1)}) %all-gather.3.cloned.1.call-update) | async-done | bytes 4194320 | tf_op jit(solution)/shard_map/all_gather | solution.py:46
  127.0 6.8 %select_reduce_fusion = (f32[256]{0:T(256)S(1)}, f32[256]{0:T(256)S(1)}, f32[256,4096]{1,0:T(8,128)}) fusion(s32[256]{0:T(256)S(1)} %get-tuple-element.11, s32[256]{0:T(256)S(1)} %get-tuple-element.12, bf16[256,512]{0,1:T(8,128)(2,1)} %fusion.10, bf16[4096,512]{0,1:T(8,128)(2,1)} %all-gather.3.cloned.1.call-done), kind=kOutput, calls=%fused_computation.9 | convolution fusion | flops 1082129920 | bytes 8654848 | tf_op jit(solution)/shard_map/dot_general | solution.py:10
  133.8 0.6 subtract_reduce_fusion
  134.4 109.8 %psum.7 = f32[]{:T(128)} all-reduce(f32[]{:T(128)} %subtract_reduce_fusion), channel_id=1, replica_groups=mesh['group'=16,'dp'=32] {'group','dp'}, use_global_device_ids=true, to_apply=%region_5.6 | all-reduce | flops 1 | bytes 8 | tf_op jit(solution)/shard_map/psum | solution.py:55
  244.2 33.2 %all-gather = f32[16,1,256]{2,1,0:T(1,128)S(1)} all-gather(f32[1,1,256]{2,1,0:T(1,128)S(1)} %bitcast.6), channel_id=1, replica_groups=mesh['group'=16,'dp'=32] {'group'}, dimensions={0}, use_global_device_ids=true | all-gather | bytes 17408 | tf_op jit(solution)/shard_map/all_gather | solution.py:27
  277.4 0.0 copy-start
  277.4 4.0 %fusion = (bf16[256,4096]{1,0:T(8,128)(2,1)S(1)}, bf16[256,4096]{1,0:T(8,128)(2,1)S(1)}) fusion(f32[256,4096]{1,0:T(8,128)} %get-tuple-element.10, s32[256]{0:T(256)S(1)} %get-tuple-element.11, f32[256]{0:T(256)S(1)} %get-tuple-element.7, s32[256]{0:T(256)S(1)} %get-tuple-element.12, f32[4096]{0:T(1024)S(1)} %bitcast.5), kind=kLoop, calls=%fused_computation.3 | loop fusion | flops 11534336 | bytes 8408064 | tf_op jit(solution)/shard_map/convert_element_type | solution.py:18
  281.4 0.0 copy-done
  281.4 2.4 fusion.2
  283.8 0.1 multiply_reduce_fusion
  283.9 0.1 subtract_divide_fusion
  284.1 1.0 copy.7
  (1 shorter events, 0.0 us)
Async XLA Ops:
  7.2 119.8 %all-gather.3.cloned.1.call-start = ((), (), s32[]{:S(2)}) async-start(), calls=%async_computation | async-start | bytes 4456448 | tf_op jit(solution)/shard_map/all_gather | solution.py:46
  277.4 4.0 %copy-start = (bf16[4096,512]{0,1:T(8,128)(2,1)S(1)}, bf16[4096,512]{0,1:T(8,128)(2,1)}, u32[]{:S(2)}) copy-start(bf16[4096,512]{0,1:T(8,128)(2,1)} %all-gather.3.cloned.1.call-done) | copy-start | bytes 12582916
Sparse Core Ops, SparseCore 0:
  10.6 116.3 all-gather.2
where the time goes:
time: 299 us; the launch traced here: 294 us
  blocking collectives  143 us (48%)
  waiting for transfers between devices  116 us (39%)
  between operations  15.9 us (5%)
  matrix products  9.14 us (3%)
  other arithmetic  7.55 us (3%)
    all_gather x1, waiting for transfers between devices, on_device(): batch_units = lax.all_gather(packed, 'group', axis=0, tiled=True)  116 us
    psum x1, blocking collectives, on_device(): loss_total = lax.psum(jnp.sum(loss_rows), ('group', 'dp'))  110 us
    all_gather x1, blocking collectives, share_totals(): return lax.all_gather(own_totals, 'group', axis=0, tiled=True)  33.2 us
    dot_general x1, matrix products, tile_expo(): jnp.dot(own_units, col_units.T, preferred_element_type=jnp.float32) / TAU  6.79 us
  transfers between devices with their start and end apart: 1, of which 1 were waited for; matrix products, arithmetic and copies ran while one was open for 0% of the time, Pallas kernels for 0%

commit v1 on v0

v1 whole, which is shorter than its diff:
```python
import functools

import jax
import jax.numpy as jnp
from jax import lax
from jax.experimental import pallas as pl
from jax.experimental.pallas import tpu as pltpu
from jax.sharding import PartitionSpec as P

TAU = 0.1
LOG2E = 1.4426950408889634
SCALE = LOG2E / TAU
X = 4
Z = 4
B = 256
E = 512
SLOTS = X * Z
ORDER = [
    (0, 0), (0, 1), (0, 2), (0, 3),
    (1, 0), (1, 1), (3, 0), (3, 1),
    (1, 2), (1, 3), (3, 2), (3, 3),
    (2, 0), (2, 1),
    (2, 2), (2, 3),
]
STAGES = (4, 8, 12, 14, 16)
CHUNK = 1024
MIB = 1024 * 1024
VMEM = pl.BlockSpec(memory_space=pltpu.VMEM)
HBM = pl.BlockSpec(memory_space=pltpu.HBM)


def nt_dot(a, b):
    return lax.dot_general(a, b, (((1,), (1,)), ((), ())), preferred_element_type=jnp.float32)


def column(row):
    return jnp.broadcast_to(row, (128, B)).T


def pack_kernel(emb_ref, packed_ref):
    emb = emb_ref[...]
    lengths = jnp.sqrt(jnp.sum(emb * emb, axis=1, keepdims=True) + 1e-06)
    packed_ref[...] = (emb / lengths).astype(jnp.bfloat16)


def pack(embeddings):
    return pl.pallas_call(
        pack_kernel,
        out_shape=jax.ShapeDtypeStruct((B, E), jnp.bfloat16),
        in_specs=[VMEM],
        out_specs=VMEM,
        compiler_params=pltpu.CompilerParams(vmem_limit_bytes=4 * MIB),
    )(embeddings)


def owners():
    group_pos = lax.axis_index("group")
    own_x, own_z = lax.div(group_pos, Z), lax.rem(group_pos, Z)
    way = 1 - 2 * lax.rem(lax.axis_index("dp"), 2)
    return [((own_x - way * back_x) & (X - 1)) * Z + (own_z ^ mask) for back_x, mask in ORDER]


def place_kernel(dp_count, partner_ref, place_ref, own_ref, near, sem):
    group_pos = lax.axis_index("group")
    own_x, own_z = lax.div(group_pos, Z), lax.rem(group_pos, Z)
    lines = B // 128
    starts = [(owner * dp_count + lax.axis_index("dp")) * lines for owner in owners()]
    bases = [pl.multiple_of(lax.div(start, 8) * 8, 8) for start in starts]
    copies = [
        pltpu.make_async_copy(partner_ref.at[pl.ds(base, 8), :], near.at[k], sem.at[k])
        for k, base in enumerate(bases)
    ]
    for copy in copies:
        copy.start()
    for copy in copies:
        copy.wait()
    for s in range(SLOTS):
        for line in range(lines):
            row = near[s, pl.ds(starts[s] - bases[s] + line, 1), :]
            place_ref[s : s + 1, line * 128 : (line + 1) * 128] = row
    partner = place_ref[...]
    far = partner // (dp_count * B)
    way = 1 - 2 * lax.rem(lax.axis_index("dp"), 2)
    back = ((way * (own_x - far // Z)) & (X - 1)) * Z + ((far & (Z - 1)) ^ own_z)
    slot = jnp.zeros_like(back)
    for k, (back_x, mask) in enumerate(ORDER):
        slot = jnp.where(back == back_x * Z + mask, k, slot)
    place = slot * B + (partner & (B - 1))
    place_ref[...] = place
    own_ref[...] = column(place[0:1, :])


def places(partner, dp_count):
    return pl.pallas_call(
        functools.partial(place_kernel, dp_count),
        out_shape=(
            jax.ShapeDtypeStruct((SLOTS, B), jnp.int32),
            jax.ShapeDtypeStruct((B, 128), jnp.int32),
        ),
        in_specs=[HBM],
        out_specs=(VMEM, VMEM),
        scratch_shapes=[pltpu.VMEM((SLOTS, 8, 128), jnp.int32), pltpu.SemaphoreType.DMA((SLOTS,))],
        compiler_params=pltpu.CompilerParams(vmem_limit_bytes=4 * MIB),
    )(pltpu.with_memory_space_constraint(partner.reshape(-1, 128), pltpu.HBM))


def split_blocks(pieces):
    return [(piece, row) for piece in pieces for row in range(0, piece.shape[0], B)]


def sums_kernel(first, last, n_pieces, n_old, *refs):
    pieces = refs[:n_pieces]
    place_ref = refs[n_pieces]
    sums_in = refs[n_pieces + 1] if first > 0 else None
    sums_out, units_out, *part_out, sem = refs[n_pieces + (2 if first > 0 else 1) :]
    copies, done = [], 0
    for k, piece in enumerate(pieces[n_old:]):
        rows = piece.shape[0]
        copies.append(pltpu.make_async_copy(piece, units_out.at[pl.ds(done, rows), :], sem.at[k]))
        done += rows
    for copy in copies:
        copy.start()
    blocks = [piece[row : row + B, :] for piece, row in split_blocks(pieces)]
    rows = lax.broadcasted_iota(jnp.int32, (B, B), 0)
    lanes = lax.broadcasted_iota(jnp.int32, (B, B), 1)
    place = place_ref[...]

    def fold(value):
        return jnp.sum(value.reshape(B // 8, 8, B), axis=0)

    sums = [jnp.zeros((8, B), jnp.float32)] * last
    hits = jnp.zeros((8, B), jnp.float32)
    row_sums = {}
    for a in range(first, last):
        total = jnp.zeros((B, 128), jnp.float32)
        for c in [*range(first), *range(a, last)]:
            raw = nt_dot(blocks[a], blocks[c])
            e = jnp.exp2(raw * SCALE)
            if c == a:
                e = jnp.where(rows == lanes, 0.0, e)
            total = total + (e[:, :128] + e[:, 128:])
            found = fold(jnp.where(rows == place[c : c + 1, :] - a * B, raw, 0.0))
            if c != a:
                sums[c] = sums[c] + fold(e)
                found = 2.0 * found
            hits = hits + found
        row_sums[a] = jnp.sum(total.T, axis=0, keepdims=True)
    for s in range(last):
        total = jnp.sum(sums[s], axis=0, keepdims=True)
        total = total + (sums_in[s : s + 1, :] if s < first else row_sums[s])
        sums_out[s : s + 1, :] = total
    if last < SLOTS:
        sums_out[last:SLOTS, :] = jnp.zeros((SLOTS - last, B), jnp.float32)
    if first > 0:
        hits = hits + sums_in[SLOTS:, :]
    sums_out[SLOTS:, :] = hits
    if last == SLOTS:
        logs = jnp.log(sums_out[:SLOTS, :])
        part = jnp.sum(logs, axis=0, keepdims=True) - jnp.sum(hits, axis=0, keepdims=True) * (1.0 / TAU)
        part = part[:, :128] + part[:, 128:]
        part_out[0][...] = jnp.broadcast_to(part[None], part_out[0].shape)
    for copy in copies:
        copy.wait()


def sums(first, last, old, new, place, state, dp_count):
    pairs = (last - first) * (last + first + 1) // 2
    operands = list(old) + list(new) + [place] + list(state)
    is_last = last == SLOTS
    return pl.pallas_call(
        functools.partial(sums_kernel, first, last, len(old) + len(new), len(old)),
        out_shape=(
            jax.ShapeDtypeStruct((SLOTS + 8, B), jnp.float32),
            pltpu.HBM(((last - first) * B, E), jnp.bfloat16),
        )
        + ((jax.ShapeDtypeStruct((dp_count, 1, 128), jnp.float32),) if is_last else ()),
        in_specs=[VMEM] * len(operands),
        out_specs=(VMEM, HBM) + ((VMEM,) if is_last else ()),
        scratch_shapes=[pltpu.SemaphoreType.DMA((len(new),))],
        compiler_params=pltpu.CompilerParams(vmem_limit_bytes=12 * MIB),
        cost_estimate=pl.CostEstimate(
            flops=pairs * 2 * B * B * E, bytes_accessed=last * B * E * 2, transcendentals=pairs * B * B
        ),
    )(*operands)


def grad_kernel(*refs):
    unit_refs = refs[: len(STAGES)]
    place_ref, totals_ref, emb_ref, grad_ref, units, sem = refs[len(STAGES) :]
    copies = []
    for k, (ref, row) in enumerate(split_blocks(unit_refs)):
        target = units.at[pl.ds(k * B, B), :]
        copies.append(pltpu.make_async_copy(ref.at[pl.ds(row, B), :], target, sem.at[k]))
    for copy in copies:
        copy.start()
    inverse = 1.0 / totals_ref[:SLOTS, :]
    row_inv = column(inverse[0:1, :])
    row_inv = jnp.concatenate([row_inv, row_inv], axis=1)
    place = jnp.concatenate([place_ref[...], place_ref[...]], axis=1)
    rows = lax.broadcasted_iota(jnp.int32, (B, B), 0)
    lanes = lax.broadcasted_iota(jnp.int32, (B, B), 1)
    emb = emb_ref[...]
    lengths = jnp.sqrt(jnp.sum(emb * emb, axis=1, keepdims=True) + 1e-06)
    unit = emb / lengths
    unit_grad = None
    for start in range(0, SLOTS * B, CHUNK):
        for copy in copies[start // B : (start + CHUNK) // B]:
            copy.wait()
        cols = units[start : start + CHUNK, :]
        raw = nt_dot(units[0:B, :], cols)
        row_w, col_w = [], []
        for k in range(CHUNK // B):
            b = start // B + k
            e = jnp.exp2(raw[:, k * B : (k + 1) * B] * SCALE)
            if b == 0:
                e = jnp.where(rows == lanes, 0.0, e)
            ind = jnp.where(lanes + b * B == place, 1.0, 0.0)
            row_w.append((e * row_inv - ind).astype(jnp.bfloat16))
            col_w.append((e * inverse[b : b + 1, :] - ind).astype(jnp.bfloat16))
        both = jnp.concatenate(
            [jnp.concatenate(row_w, axis=1), jnp.concatenate(col_w, axis=1)], axis=0
        )
        both = jnp.dot(both, cols, preferred_element_type=jnp.float32)
        part = both[:B] + both[B:]
        unit_grad = part if unit_grad is None else unit_grad + part
    unit_grad = unit_grad * (1.0 / TAU)
    along = jnp.sum(unit * unit_grad, axis=1, keepdims=True)
    grad_ref[...] = (unit_grad - unit * along) / lengths


def grads(units, place, totals, embeddings):
    return pl.pallas_call(
        grad_kernel,
        out_shape=jax.ShapeDtypeStruct((B, E), jnp.float32),
        in_specs=[HBM] * len(units) + [VMEM] * 3,
        out_specs=VMEM,
        scratch_shapes=[
            pltpu.VMEM((SLOTS * B, E), jnp.bfloat16),
            pltpu.SemaphoreType.DMA((SLOTS,)),
        ],
        compiler_params=pltpu.CompilerParams(vmem_limit_bytes=16 * MIB),
        cost_estimate=pl.CostEstimate(
            flops=6 * SLOTS * B * B * E, bytes_accessed=SLOTS * B * E * 2, transcendentals=SLOTS * B * B
        ),
    )(*[pltpu.with_memory_space_constraint(part, pltpu.HBM) for part in units], place, totals, embeddings)


def shift_x(value, step):
    dp_count = lax.axis_size("dp")
    perm = []
    for x in range(X):
        for z in range(Z):
            for k in range(dp_count):
                to_x = (x + (step if k % 2 == 0 else -step)) % X
                perm.append(((x * Z + z) * dp_count + k, (to_x * Z + z) * dp_count + k))
    return lax.ppermute(value, ("group", "dp"), perm)


def swap_z(value, mask):
    perm = [(x * Z + z, x * Z + (z ^ mask)) for x in range(X) for z in range(Z)]
    return lax.ppermute(value, "group", perm)


def stack_kernel(first_ref, second_ref, both_ref):
    both_ref[:B, :] = first_ref[...]
    both_ref[B:, :] = second_ref[...]


def stack(first, second):
    return pl.pallas_call(
        stack_kernel,
        out_shape=jax.ShapeDtypeStruct((2 * B, E), jnp.bfloat16),
        in_specs=[VMEM, VMEM],
        out_specs=VMEM,
        compiler_params=pltpu.CompilerParams(vmem_limit_bytes=4 * MIB),
    )(first, second)


def on_device(embeddings, partner):
    dp_count = lax.axis_size("dp")
    group_count = lax.axis_size("group")
    packed = pack(embeddings)
    place, own_place = places(partner, dp_count)

    z1 = swap_z(packed, 1)
    z2 = swap_z(packed, 2)
    near = stack(packed, z1)
    near_1, near_3 = shift_x(near, 1), shift_x(near, 3)
    z3, place, own_place = lax.optimization_barrier((swap_z(z2, 1), place, own_place))
    far = stack(z2, z3)
    far_1, far_3 = shift_x(far, 1), shift_x(far, 3)

    old, units, state = [], [], ()

    def add(*new):
        first, last = sum(STAGES[len(units) - 1 : len(units)]), STAGES[len(units)]
        part_sums, part_units, *rest = sums(first, last, old, new, place, state, dp_count)
        units.append(part_units)
        old.extend(new)
        return (part_sums,), rest

    state, _ = add(near, far)
    state, _ = add(near_1, near_3)
    near_1, near_3, *state = lax.optimization_barrier((near_1, near_3, *state))
    near_2 = shift_x(near_1, 1)
    far_3, *state = lax.optimization_barrier((far_3, *state))
    far_2 = shift_x(far_3, 3)
    state, _ = add(far_1, far_3)
    state, _ = add(near_2)
    (totals,), (part,) = add(far_2)
    losses = lax.all_to_all(part, "dp", 0, 0)
    gradient = grads(units, own_place, totals, embeddings)
    loss = jnp.sum(losses) / (B * dp_count * group_count)
    return (gradient, loss)


def solution(mesh):
    placed = (P(("group", "dp"), None), P())
    return jax.shard_map(
        on_device,
        mesh=mesh,
        in_specs=placed,
        out_specs=(P(("group", "dp"), None), P()),
        check_vma=False,
    )
```

time: 299 us -> 101 us (0.34); the launches traced: 294 us -> 101 us
  blocking collectives: 143 us -> 0 us
  waiting for transfers between devices: 116 us -> 19.3 us
  starting transfers between devices: 0.04 us -> 54.1 us
  Pallas kernels: 0 us -> 22.9 us
  between operations: 15.9 us -> 2.62 us
  matrix products: 9.14 us -> 0 us
  other arithmetic: 7.55 us -> 0.63 us
    all_gather x1 -> x0, waiting for transfers between devices: 116 us -> none  [on_device(): batch_units = lax.all_gather(packed, 'group', axis=0, tiled=True)]
    psum x1 -> x0, blocking collectives: 110 us -> none  [on_device(): loss_total = lax.psum(jnp.sum(loss_rows), ('group', 'dp'))]
    ppermute x0 -> x9, starting transfers between devices: none -> 35.2 us  [the longest x6 22.8 us: shift_x(): return lax.ppermute(value, ('group', 'dp'), perm)]
    all_gather x1 -> x0, blocking collectives: 33.2 us -> none  [share_totals(): return lax.all_gather(own_totals, 'group', axis=0, tiled=True)]
    pallas_call x0 -> x10, Pallas kernels: none -> 22.9 us  [the longest x5 15.4 us: sums(): pl.pallas_call(functools.partial(sums_kernel, first, last, len(old) + len...]
    all_to_all x0 -> x1, starting transfers between devices: none -> 18.8 us  [on_device(): losses = lax.all_to_all(part, 'dp', 0, 0)]
    ppermute x0 -> x9, waiting for transfers between devices: none -> 11.2 us  [the longest x6 7.15 us: shift_x(): return lax.ppermute(value, ('group', 'dp'), perm)]
    dot_general x2 -> x0, matrix products: 9.14 us -> none  [the longest x1 6.79 us: tile_expo(): jnp.dot(own_units, col_units.T, preferred_element_type=jnp.float32) / TAU]
  transfers between devices with their start and end apart: 1 -> 10, of which waited for: 1 -> 5; matrix products, arithmetic and copies ran while one was open for 0% -> 0% of each run, Pallas kernels for 0% -> 19%
where the time goes in v1:
time: 101 us
  starting transfers between devices  54.1 us (54%)
  Pallas kernels  22.9 us (23%)
  waiting for transfers between devices  19.3 us (19%)
  between operations  2.62 us (3%)
  local copies, waits for them, and re-layouts  1.04 us (1%)
    ppermute x6, starting transfers between devices, shift_x(): return lax.ppermute(value, ('group', 'dp'), perm)  22.8 us
    all_to_all x1, starting transfers between devices, on_device(): losses = lax.all_to_all(part, 'dp', 0, 0)  18.8 us
    pallas_call x5, Pallas kernels, sums(): pl.pallas_call(functools.partial(sums_kernel, first, last, len(old) + len...  15.4 us
    ppermute x3, starting transfers between devices, swap_z(): return lax.ppermute(value, 'group', perm)  12.4 us
    all_to_all x1, waiting for transfers between devices, on_device(): losses = lax.all_to_all(part, 'dp', 0, 0)  8.1 us
    ppermute x6, waiting for transfers between devices, shift_x(): return lax.ppermute(value, ('group', 'dp'), perm)  7.15 us
    pallas_call x1, Pallas kernels, grads(): pl.pallas_call(grad_kernel, out_shape=jax.ShapeDtypeStruct((B, E), jnp.fl...  6.05 us
    ppermute x3, waiting for transfers between devices, swap_z(): return lax.ppermute(value, 'group', perm)  4.08 us
  transfers between devices with their start and end apart: 10, of which 5 were waited for; matrix products, arithmetic and copies ran while one was open for 0% of the time, Pallas kernels for 19%

profile of v1, /device:TPU:1, one launch (start us, length us, event | category | flops | bytes accessed | tf_op | source)
XLA Modules:
  0.0 100.6 jit_solution(5654992937047550763)
XLA Ops:
  0.6 0.0 copy-start
  0.6 1.0 %copy-done = f32[256,512]{1,0:T(8,128)S(1)} copy-done((f32[256,512]{1,0:T(8,128)S(1)}, f32[256,512]{1,0:T(8,128)}, u32[]{:S(2)}) %copy-start) | copy-done | bytes 524312
  1.7 0.1 shard_map.41.first_ref
  1.8 4.4 %collective-permute-start = (bf16[256,512]{1,0:T(8,128)(2,1)S(1)}, bf16[256,512]{1,0:T(8,128)(2,1)S(1)}, u32[]{:S(2)}, u32[]{:S(2)}) collective-permute-start(bf16[256,512]{1,0:T(8,128)(2,1)S(1)} %shard_map.41.first_ref), channel_id=1, source_target_pairs={{0,32},{32,0},{64,96},{96,64},{128,160},{160,128},{192,224},{224,1... | collective-permute-start | bytes 786440 | tf_op jit(solution)/shard_map/ppermute | solution.py:261
  6.2 4.9 %collective-permute-start.1 = (bf16[256,512]{1,0:T(8,128)(2,1)S(1)}, bf16[256,512]{1,0:T(8,128)(2,1)S(1)}, u32[]{:S(2)}, u32[]{:S(2)}) collective-permute-start(bf16[256,512]{1,0:T(8,128)(2,1)S(1)} %shard_map.41.first_ref), channel_id=1, source_target_pairs={{0,64},{32,96},{64,0},{96,32},{128,192},{160,224},{192,128},{224,1... | collective-permute-start | bytes 786440 | tf_op jit(solution)/shard_map/ppermute | solution.py:261
  11.1 0.0 collective-permute-done.second_ref
  11.2 4.1 %collective-permute-start.4 = (bf16[512,512]{1,0:T(8,128)(2,1)S(1)}, bf16[512,512]{1,0:T(8,128)(2,1)S(1)}, u32[]{:S(2)}, u32[]{:S(2)}) collective-permute-start(bf16[512,512]{1,0:T(8,128)(2,1)S(1)} %shard_map.42.refs_0_), channel_id=1, source_target_pairs={{0,384},{1,129},{2,386},{3,131},{4,388},{5,133},{6,390},{7,135},{8... | collective-permute-start | bytes 1572872 | tf_op jit(solution)/shard_map/ppermute | solution.py:256
  15.3 3.2 %collective-permute-start.3 = (bf16[512,512]{1,0:T(8,128)(2,1)S(1)}, bf16[512,512]{1,0:T(8,128)(2,1)S(1)}, u32[]{:S(2)}, u32[]{:S(2)}) collective-permute-start(bf16[512,512]{1,0:T(8,128)(2,1)S(1)} %shard_map.42.refs_0_), channel_id=1, source_target_pairs={{0,128},{1,385},{2,130},{3,387},{4,132},{5,389},{6,134},{7,391},{8... | collective-permute-start | bytes 1572872 | tf_op jit(solution)/shard_map/ppermute | solution.py:256
  18.5 0.0 collective-permute-done.1.first_ref
  18.5 3.2 %collective-permute-start.2 = (bf16[256,512]{1,0:T(8,128)(2,1)S(1)}, bf16[256,512]{1,0:T(8,128)(2,1)S(1)}, u32[]{:S(2)}, u32[]{:S(2)}) collective-permute-start(bf16[256,512]{1,0:T(8,128)(2,1)S(1)} %collective-permute-done.1.first_ref), channel_id=1, source_target_pairs={{0,32},{32,0},{64,96},{96,64},{128,160},{160,128},{192,224},{224,1... | collective-permute-start | bytes 786440 | tf_op jit(solution)/shard_map/ppermute | solution.py:261
  21.7 1.2 %shard_map.43 = (s32[16,256]{1,0:T(8,128)S(1)}, s32[256,128]{1,0:T(8,128)S(1)}) custom-call(s32[1024,128]{1,0:T(8,128)} %bitcast.1), custom_call_target="tpu_custom_call" | custom-call | tf_op jit(solution)/shard_map/pallas_call | solution.py:94
  22.9 4.1 %collective-permute-done.2.second_ref = bf16[256,512]{1,0:T(8,128)(2,1)S(1)} collective-permute-done((bf16[256,512]{1,0:T(8,128)(2,1)S(1)}, bf16[256,512]{1,0:T(8,128)(2,1)S(1)}, u32[]{:S(2)}, u32[]{:S(2)}) %collective-permute-start.2) | collective-permute-done | bytes 262176 | tf_op jit(solution)/shard_map/ppermute | solution.py:261
  27.0 6.9 %collective-permute-start.6 = (bf16[512,512]{1,0:T(8,128)(2,1)S(1)}, bf16[512,512]{1,0:T(8,128)(2,1)S(1)}, u32[]{:S(2)}, u32[]{:S(2)}) collective-permute-start(bf16[512,512]{1,0:T(8,128)(2,1)S(1)} %shard_map.44.refs_1_), channel_id=1, source_target_pairs={{0,384},{1,129},{2,386},{3,131},{4,388},{5,133},{6,390},{7,135},{8... | collective-permute-start | bytes 1572872 | tf_op jit(solution)/shard_map/ppermute | solution.py:256
  33.9 3.2 %collective-permute-start.5 = (bf16[512,512]{1,0:T(8,128)(2,1)S(1)}, bf16[512,512]{1,0:T(8,128)(2,1)S(1)}, u32[]{:S(2)}, u32[]{:S(2)}) collective-permute-start(bf16[512,512]{1,0:T(8,128)(2,1)S(1)} %shard_map.44.refs_1_), channel_id=1, source_target_pairs={{0,128},{1,385},{2,130},{3,387},{4,132},{5,389},{6,134},{7,391},{8... | collective-permute-start | bytes 1572872 | tf_op jit(solution)/shard_map/ppermute | solution.py:256
  37.1 1.2 %shard_map.45 = (f32[24,256]{1,0:T(8,128)S(1)}, bf16[1024,512]{1,0:T(8,128)(2,1)}) custom-call(bf16[512,512]{1,0:T(8,128)(2,1)S(1)} %shard_map.42.refs_0_, bf16[512,512]{1,0:T(8,128)(2,1)S(1)} %shard_map.44.refs_1_, s32[16,256]{1,0:T(8,128)S(1)} %get-tuple-element.25.refs_2_.refs_4_.refs_6_.refs_7_.refs_8_), custom_call_target="tpu_custom_call" | custom-call | flops 671088640 | bytes 1048576 | tf_op jit(solution)/shard_map/pallas_call | solution.py:170
  38.3 0.0 collective-permute-done.4.refs_3_
  38.3 0.0 collective-permute-done.3.refs_2_
  38.3 3.4 %shard_map.46 = (f32[24,256]{1,0:T(8,128)S(1)}, bf16[1024,512]{1,0:T(8,128)(2,1)}) custom-call(bf16[512,512]{1,0:T(8,128)(2,1)S(1)} %shard_map.42.refs_0_, bf16[512,512]{1,0:T(8,128)(2,1)S(1)} %shard_map.44.refs_1_, bf16[512,512]{1,0:T(8,128)(2,1)S(1)} %collective-permute-done.3.refs_2_, bf16[512,512]{1,0:T(8,128)(2,1)S(1)} %collective-permute-done.4.refs_3_, ...), custom_call_target="tpu_custom_call" | custom-call | flops 1744830464 | bytes 2097152 | tf_op jit(solution)/shard_map/pallas_call | solution.py:170
  41.7 3.4 %collective-permute-start.7 = (bf16[512,512]{1,0:T(8,128)(2,1)S(1)}, bf16[512,512]{1,0:T(8,128)(2,1)S(1)}, u32[]{:S(2)}, u32[]{:S(2)}) collective-permute-start(bf16[512,512]{1,0:T(8,128)(2,1)S(1)} %collective-permute-done.3.refs_2_), channel_id=1, source_target_pairs={{0,128},{1,385},{2,130},{3,387},{4,132},{5,389},{6,134},{7,391},{8... | collective-permute-start | bytes 1572872 | tf_op jit(solution)/shard_map/ppermute | solution.py:256
  45.0 0.0 collective-permute-done.6.refs_5_
  45.1 2.1 %collective-permute-start.8 = (bf16[512,512]{1,0:T(8,128)(2,1)S(1)}, bf16[512,512]{1,0:T(8,128)(2,1)S(1)}, u32[]{:S(2)}, u32[]{:S(2)}) collective-permute-start(bf16[512,512]{1,0:T(8,128)(2,1)S(1)} %collective-permute-done.6.refs_5_), channel_id=1, source_target_pairs={{0,384},{1,129},{2,386},{3,131},{4,388},{5,133},{6,390},{7,135},{8... | collective-permute-start | bytes 1572872 | tf_op jit(solution)/shard_map/ppermute | solution.py:256
  47.2 2.1 %collective-permute-done.5.refs_4_ = bf16[512,512]{1,0:T(8,128)(2,1)S(1)} collective-permute-done((bf16[512,512]{1,0:T(8,128)(2,1)S(1)}, bf16[512,512]{1,0:T(8,128)(2,1)S(1)}, u32[]{:S(2)}, u32[]{:S(2)}) %collective-permute-start.5) | collective-permute-done | bytes 524320 | tf_op jit(solution)/shard_map/ppermute | solution.py:256
  49.2 4.7 %shard_map.47 = (f32[24,256]{1,0:T(8,128)S(1)}, bf16[1024,512]{1,0:T(8,128)(2,1)}) custom-call(bf16[512,512]{1,0:T(8,128)(2,1)S(1)} %shard_map.42.refs_0_, bf16[512,512]{1,0:T(8,128)(2,1)S(1)} %shard_map.44.refs_1_, bf16[512,512]{1,0:T(8,128)(2,1)S(1)} %collective-permute-done.3.refs_2_, bf16[512,512]{1,0:T(8,128)(2,1)S(1)} %collective-permute-done.4.refs_3_, ...), custom_call_target="tpu_custom_call" | custom-call | flops 2818572288 | bytes 3145728 | tf_op jit(solution)/shard_map/pallas_call | solution.py:170
  53.9 0.9 collective-permute-done.7.refs_6_
  54.8 2.6 %shard_map.48 = (f32[24,256]{1,0:T(8,128)S(1)}, bf16[512,512]{1,0:T(8,128)(2,1)}) custom-call(bf16[512,512]{1,0:T(8,128)(2,1)S(1)} %shard_map.42.refs_0_, bf16[512,512]{1,0:T(8,128)(2,1)S(1)} %shard_map.44.refs_1_, bf16[512,512]{1,0:T(8,128)(2,1)S(1)} %collective-permute-done.3.refs_2_, bf16[512,512]{1,0:T(8,128)(2,1)S(1)} %collective-permute-done.4.refs_3_, ...), custom_call_target="tpu_custom_call" | custom-call | flops 1811939328 | bytes 3670016 | tf_op jit(solution)/shard_map/pallas_call | solution.py:170
  57.5 4.2 %collective-permute-done.8.refs_7_ = bf16[512,512]{1,0:T(8,128)(2,1)S(1)} collective-permute-done((bf16[512,512]{1,0:T(8,128)(2,1)S(1)}, bf16[512,512]{1,0:T(8,128)(2,1)S(1)}, u32[]{:S(2)}, u32[]{:S(2)}) %collective-permute-start.8) | collective-permute-done | bytes 524320 | tf_op jit(solution)/shard_map/ppermute | solution.py:256
  61.7 0.0 copy-start.1
  61.7 3.5 %shard_map.49 = (f32[24,256]{1,0:T(8,128)S(1)}, bf16[512,512]{1,0:T(8,128)(2,1)}, f32[32,1,128]{2,1,0:T(1,128)}) custom-call(bf16[512,512]{1,0:T(8,128)(2,1)S(1)} %shard_map.42.refs_0_, bf16[512,512]{1,0:T(8,128)(2,1)S(1)} %shard_map.44.refs_1_, bf16[512,512]{1,0:T(8,128)(2,1)S(1)} %collective-permute-done.3.refs_2_, ...), custom_call_target="tpu_custom_call" | custom-call | flops 2080374784 | bytes 4194304 | tf_op jit(solution)/shard_map/pallas_call | solution.py:170
  65.2 18.8 %all-to-all-start = ((f32[32,1,128]{2,1,0:T(1,128)}), f32[32,1,128]{2,1,0:T(1,128)S(1)}, u32[]{:S(2)}, u32[]{:S(2)}) async-start(f32[32,1,128]{2,1,0:T(1,128)} %get-tuple-element.41), calls=%async_computation | async-start | bytes 32768 | tf_op jit(solution)/shard_map/all_to_all | solution.py:311
  84.0 0.0 copy-done.1
  84.0 6.1 %shard_map.50 = f32[256,512]{1,0:T(8,128)} custom-call(bf16[1024,512]{1,0:T(8,128)(2,1)} %get-tuple-element.26.refs_0_, bf16[1024,512]{1,0:T(8,128)(2,1)} %get-tuple-element.28.refs_1_, bf16[1024,512]{1,0:T(8,128)(2,1)} %get-tuple-element.33.refs_2_, bf16[512,512]{1,0:T(8,128)(2,1)} %get-tuple-element.36.refs_3_, ...), custom_call_target="tpu_custom_call" | custom-call | flops 3221225472 | bytes 4194304 | tf_op jit(solution)/shard_map/pallas_call | solution.py:232
  90.1 8.1 %all-to-all-done = f32[32,1,128]{2,1,0:T(1,128)S(1)} async-done(((f32[32,1,128]{2,1,0:T(1,128)}), f32[32,1,128]{2,1,0:T(1,128)S(1)}, u32[]{:S(2)}, u32[]{:S(2)}) %all-to-all-start) | async-done | bytes 16416 | tf_op jit(solution)/shard_map/all_to_all | solution.py:311
  98.2 0.6 reduce_sum.9
  (2 shorter events, 0.1 us)
Async XLA Ops:
  0.6 1.0 %copy-start = (f32[256,512]{1,0:T(8,128)S(1)}, f32[256,512]{1,0:T(8,128)}, u32[]{:S(2)}) copy-start(f32[256,512]{1,0:T(8,128)} %refs_7_.1) | copy-start | bytes 1572868
  1.8 9.3 %collective-permute-start = (bf16[256,512]{1,0:T(8,128)(2,1)S(1)}, bf16[256,512]{1,0:T(8,128)(2,1)S(1)}, u32[]{:S(2)}, u32[]{:S(2)}) collective-permute-start(bf16[256,512]{1,0:T(8,128)(2,1)S(1)} %shard_map.41.first_ref), channel_id=1, source_target_pairs={{0,32},{32,0},{64,96},{96,64},{128,160},{160,128},{192,224},{224,1... | collective-permute-start | bytes 786440 | tf_op jit(solution)/shard_map/ppermute | solution.py:261
  6.2 12.3 %collective-permute-start.1 = (bf16[256,512]{1,0:T(8,128)(2,1)S(1)}, bf16[256,512]{1,0:T(8,128)(2,1)S(1)}, u32[]{:S(2)}, u32[]{:S(2)}) collective-permute-start(bf16[256,512]{1,0:T(8,128)(2,1)S(1)} %shard_map.41.first_ref), channel_id=1, source_target_pairs={{0,64},{32,96},{64,0},{96,32},{128,192},{160,224},{192,128},{224,1... | collective-permute-start | bytes 786440 | tf_op jit(solution)/shard_map/ppermute | solution.py:261
  11.2 27.1 %collective-permute-start.4 = (bf16[512,512]{1,0:T(8,128)(2,1)S(1)}, bf16[512,512]{1,0:T(8,128)(2,1)S(1)}, u32[]{:S(2)}, u32[]{:S(2)}) collective-permute-start(bf16[512,512]{1,0:T(8,128)(2,1)S(1)} %shard_map.42.refs_0_), channel_id=1, source_target_pairs={{0,384},{1,129},{2,386},{3,131},{4,388},{5,133},{6,390},{7,135},{8... | collective-permute-start | bytes 1572872 | tf_op jit(solution)/shard_map/ppermute | solution.py:256
  15.3 23.0 %collective-permute-start.3 = (bf16[512,512]{1,0:T(8,128)(2,1)S(1)}, bf16[512,512]{1,0:T(8,128)(2,1)S(1)}, u32[]{:S(2)}, u32[]{:S(2)}) collective-permute-start(bf16[512,512]{1,0:T(8,128)(2,1)S(1)} %shard_map.42.refs_0_), channel_id=1, source_target_pairs={{0,128},{1,385},{2,130},{3,387},{4,132},{5,389},{6,134},{7,391},{8... | collective-permute-start | bytes 1572872 | tf_op jit(solution)/shard_map/ppermute | solution.py:256
  18.5 8.5 %collective-permute-start.2 = (bf16[256,512]{1,0:T(8,128)(2,1)S(1)}, bf16[256,512]{1,0:T(8,128)(2,1)S(1)}, u32[]{:S(2)}, u32[]{:S(2)}) collective-permute-start(bf16[256,512]{1,0:T(8,128)(2,1)S(1)} %collective-permute-done.1.first_ref), channel_id=1, source_target_pairs={{0,32},{32,0},{64,96},{96,64},{128,160},{160,128},{192,224},{224,1... | collective-permute-start | bytes 786440 | tf_op jit(solution)/shard_map/ppermute | solution.py:261
  27.0 18.1 %collective-permute-start.6 = (bf16[512,512]{1,0:T(8,128)(2,1)S(1)}, bf16[512,512]{1,0:T(8,128)(2,1)S(1)}, u32[]{:S(2)}, u32[]{:S(2)}) collective-permute-start(bf16[512,512]{1,0:T(8,128)(2,1)S(1)} %shard_map.44.refs_1_), channel_id=1, source_target_pairs={{0,384},{1,129},{2,386},{3,131},{4,388},{5,133},{6,390},{7,135},{8... | collective-permute-start | bytes 1572872 | tf_op jit(solution)/shard_map/ppermute | solution.py:256
  33.9 15.4 %collective-permute-start.5 = (bf16[512,512]{1,0:T(8,128)(2,1)S(1)}, bf16[512,512]{1,0:T(8,128)(2,1)S(1)}, u32[]{:S(2)}, u32[]{:S(2)}) collective-permute-start(bf16[512,512]{1,0:T(8,128)(2,1)S(1)} %shard_map.44.refs_1_), channel_id=1, source_target_pairs={{0,128},{1,385},{2,130},{3,387},{4,132},{5,389},{6,134},{7,391},{8... | collective-permute-start | bytes 1572872 | tf_op jit(solution)/shard_map/ppermute | solution.py:256
  41.7 13.2 %collective-permute-start.7 = (bf16[512,512]{1,0:T(8,128)(2,1)S(1)}, bf16[512,512]{1,0:T(8,128)(2,1)S(1)}, u32[]{:S(2)}, u32[]{:S(2)}) collective-permute-start(bf16[512,512]{1,0:T(8,128)(2,1)S(1)} %collective-permute-done.3.refs_2_), channel_id=1, source_target_pairs={{0,128},{1,385},{2,130},{3,387},{4,132},{5,389},{6,134},{7,391},{8... | collective-permute-start | bytes 1572872 | tf_op jit(solution)/shard_map/ppermute | solution.py:256
  45.1 16.6 %collective-permute-start.8 = (bf16[512,512]{1,0:T(8,128)(2,1)S(1)}, bf16[512,512]{1,0:T(8,128)(2,1)S(1)}, u32[]{:S(2)}, u32[]{:S(2)}) collective-permute-start(bf16[512,512]{1,0:T(8,128)(2,1)S(1)} %collective-permute-done.6.refs_5_), channel_id=1, source_target_pairs={{0,384},{1,129},{2,386},{3,131},{4,388},{5,133},{6,390},{7,135},{8... | collective-permute-start | bytes 1572872 | tf_op jit(solution)/shard_map/ppermute | solution.py:256
  61.7 22.4 %copy-start.1 = (f32[256,512]{1,0:T(8,128)S(1)}, f32[256,512]{1,0:T(8,128)}, u32[]{:S(2)}) copy-start(f32[256,512]{1,0:T(8,128)} %refs_7_.1) | copy-start | bytes 1572868
  65.2 33.0 %all-to-all-start = ((f32[32,1,128]{2,1,0:T(1,128)}), f32[32,1,128]{2,1,0:T(1,128)S(1)}, u32[]{:S(2)}, u32[]{:S(2)}) async-start(f32[32,1,128]{2,1,0:T(1,128)} %get-tuple-element.41), calls=%async_computation | async-start | bytes 32768 | tf_op jit(solution)/shard_map/all_to_all | solution.py:311

commit v2 on v1

--- a/solution.py
+++ b/solution.py
@@ -126,25 +126,36 @@
     place = place_ref[...]
 
     def fold(value):
-        return jnp.sum(value.reshape(B // 8, 8, B), axis=0)
+        return jnp.sum(value.reshape(-1, 8, B), axis=0)
 
     sums = [jnp.zeros((8, B), jnp.float32)] * last
     hits = jnp.zeros((8, B), jnp.float32)
     row_sums = {}
-    for a in range(first, last):
-        total = jnp.zeros((B, 128), jnp.float32)
-        for c in [*range(first), *range(a, last)]:
-            raw = nt_dot(blocks[a], blocks[c])
+    for pair in range(first, last, 2):
+        both = jnp.concatenate([blocks[pair], blocks[pair + 1]], axis=0)
+        both_rows = lax.broadcasted_iota(jnp.int32, (2 * B, B), 0)
+        both_total = jnp.zeros((2 * B, 128), jnp.float32)
+        for c in range(first):
+            raw = nt_dot(both, blocks[c])
             e = jnp.exp2(raw * SCALE)
-            if c == a:
-                e = jnp.where(rows == lanes, 0.0, e)
-            total = total + (e[:, :128] + e[:, 128:])
-            found = fold(jnp.where(rows == place[c : c + 1, :] - a * B, raw, 0.0))
-            if c != a:
-                sums[c] = sums[c] + fold(e)
-                found = 2.0 * found
-            hits = hits + found
-        row_sums[a] = jnp.sum(total.T, axis=0, keepdims=True)
+            both_total = both_total + (e[:, :128] + e[:, 128:])
+            sums[c] = sums[c] + fold(e)
+            found = jnp.where(both_rows == place[c : c + 1, :] - pair * B, raw, 0.0)
+            hits = hits + 2.0 * fold(found)
+        for a in (pair, pair + 1):
+            total = both_total[(a - pair) * B : (a - pair + 1) * B, :]
+            for c in range(a, last):
+                raw = nt_dot(blocks[a], blocks[c])
+                e = jnp.exp2(raw * SCALE)
+                if c == a:
+                    e = jnp.where(rows == lanes, 0.0, e)
+                total = total + (e[:, :128] + e[:, 128:])
+                found = fold(jnp.where(rows == place[c : c + 1, :] - a * B, raw, 0.0))
+                if c != a:
+                    sums[c] = sums[c] + fold(e)
+                    found = 2.0 * found
+                hits = hits + found
+            row_sums[a] = jnp.sum(total.T, axis=0, keepdims=True)
     for s in range(last):
         total = jnp.sum(sums[s], axis=0, keepdims=True)
         total = total + (sums_in[s : s + 1, :] if s < first else row_sums[s])
@@ -287,8 +298,8 @@
     near = stack(packed, z1)
     near_1, near_3 = shift_x(near, 1), shift_x(near, 3)
     z3, place, own_place = lax.optimization_barrier((swap_z(z2, 1), place, own_place))
-    far = stack(z2, z3)
-    far_1, far_3 = shift_x(far, 1), shift_x(far, 3)
+    z2_1, z2_3 = shift_x(z2, 1), shift_x(z2, 3)
+    z3_1, z3_3 = shift_x(z3, 1), shift_x(z3, 3)
 
     old, units, state = [], [], ()
 
@@ -299,13 +310,12 @@
         old.extend(new)
         return (part_sums,), rest
 
-    state, _ = add(near, far)
+    near_1, near_3 = lax.optimization_barrier((near_1, near_3))
+    near_2 = shift_x(near_1, 1)
+    far_2 = shift_x(stack(z2_3, z3_3), 3)
+    state, _ = add(near, z2, z3)
     state, _ = add(near_1, near_3)
-    near_1, near_3, *state = lax.optimization_barrier((near_1, near_3, *state))
-    near_2 = shift_x(near_1, 1)
-    far_3, *state = lax.optimization_barrier((far_3, *state))
-    far_2 = shift_x(far_3, 3)
-    state, _ = add(far_1, far_3)
+    state, _ = add(z2_1, z3_1, z2_3, z3_3)
     state, _ = add(near_2)
     (totals,), (part,) = add(far_2)
     losses = lax.all_to_all(part, "dp", 0, 0)

time: 101 us -> 100 us (0.990)
  starting transfers between devices: 54.1 us -> 62.2 us
  waiting for transfers between devices: 19.3 us -> 12.6 us
  Pallas kernels: 22.9 us -> 20.8 us
    ppermute x6 -> x8, starting transfers between devices: 22.8 us -> 30.2 us  [shift_x(): return lax.ppermute(value, ('group', 'dp'), perm)]
    ppermute x3, waiting for transfers between devices: 4.08 us -> 0.01 us  [swap_z(): return lax.ppermute(value, 'group', perm)]
    ppermute x6 -> x8, waiting for transfers between devices: 7.15 us -> 4.56 us  [shift_x(): return lax.ppermute(value, ('group', 'dp'), perm)]
    pallas_call x5, Pallas kernels: 15.4 us -> 13.3 us  [sums(): pl.pallas_call(functools.partial(sums_kernel, first, last, len(old) + len...]
  transfers between devices with their start and end apart: 10 -> 12, of which waited for: 5 -> 2; matrix products, arithmetic and copies ran while one was open for 0% -> 0% of each run, Pallas kernels for 19% -> 17%
where the time goes in v2:
time: 100 us; the launch traced here: 99.9 us
  starting transfers between devices  62.2 us (62%)
  Pallas kernels  20.8 us (21%)
  waiting for transfers between devices  12.6 us (13%)
  between operations  2.68 us (3%)
  local copies, waits for them, and re-layouts  1.04 us (1%)
    ppermute x8, starting transfers between devices, shift_x(): return lax.ppermute(value, ('group', 'dp'), perm)  30.2 us
    all_to_all x1, starting transfers between devices, on_device(): losses = lax.all_to_all(part, 'dp', 0, 0)  19.5 us
    pallas_call x5, Pallas kernels, sums(): pl.pallas_call(functools.partial(sums_kernel, first, last, len(old) + len...  13.3 us
    ppermute x3, starting transfers between devices, swap_z(): return lax.ppermute(value, 'group', perm)  12.4 us
    all_to_all x1, waiting for transfers between devices, on_device(): losses = lax.all_to_all(part, 'dp', 0, 0)  8.08 us
    pallas_call x1, Pallas kernels, grads(): pl.pallas_call(grad_kernel, out_shape=jax.ShapeDtypeStruct((B, E), jnp.fl...  6.05 us
    ppermute x8, waiting for transfers between devices, shift_x(): return lax.ppermute(value, ('group', 'dp'), perm)  4.56 us
  transfers between devices with their start and end apart: 12, of which 2 were waited for; matrix products, arithmetic and copies ran while one was open for 0% of the time, Pallas kernels for 17%

profile of v2, /device:TPU:1, one launch (start us, length us, event | category | flops | bytes accessed | tf_op | source)
XLA Modules:
  0.0 99.9 jit_solution(11683600618848156545)
XLA Ops:
  0.6 0.0 copy-start
  0.6 1.0 %copy-done = f32[256,512]{1,0:T(8,128)S(1)} copy-done((f32[256,512]{1,0:T(8,128)S(1)}, f32[256,512]{1,0:T(8,128)}, u32[]{:S(2)}) %copy-start) | copy-done | bytes 524312
  1.7 0.1 shard_map.41.first_ref
  1.8 4.4 %collective-permute-start = (bf16[256,512]{1,0:T(8,128)(2,1)S(1)}, bf16[256,512]{1,0:T(8,128)(2,1)S(1)}, u32[]{:S(2)}, u32[]{:S(2)}) collective-permute-start(bf16[256,512]{1,0:T(8,128)(2,1)S(1)} %shard_map.41.first_ref), channel_id=1, source_target_pairs={{0,32},{32,0},{64,96},{96,64},{128,160},{160,128},{192,224},{224,1... | collective-permute-start | bytes 786440 | tf_op jit(solution)/shard_map/ppermute | solution.py:272
  6.2 4.9 %collective-permute-start.1 = (bf16[256,512]{1,0:T(8,128)(2,1)S(1)}, bf16[256,512]{1,0:T(8,128)(2,1)S(1)}, u32[]{:S(2)}, u32[]{:S(2)}) collective-permute-start(bf16[256,512]{1,0:T(8,128)(2,1)S(1)} %shard_map.41.first_ref), channel_id=1, source_target_pairs={{0,64},{32,96},{64,0},{96,32},{128,192},{160,224},{192,128},{224,1... | collective-permute-start | bytes 786440 | tf_op jit(solution)/shard_map/ppermute | solution.py:272
  11.1 0.0 collective-permute-done.second_ref
  11.2 4.1 %collective-permute-start.4 = (bf16[512,512]{1,0:T(8,128)(2,1)S(1)}, bf16[512,512]{1,0:T(8,128)(2,1)S(1)}, u32[]{:S(2)}, u32[]{:S(2)}) collective-permute-start(bf16[512,512]{1,0:T(8,128)(2,1)S(1)} %shard_map.42.refs_0_), channel_id=1, source_target_pairs={{0,384},{1,129},{2,386},{3,131},{4,388},{5,133},{6,390},{7,135},{8... | collective-permute-start | bytes 1572872 | tf_op jit(solution)/shard_map/ppermute | solution.py:267
  15.3 3.2 %collective-permute-start.3 = (bf16[512,512]{1,0:T(8,128)(2,1)S(1)}, bf16[512,512]{1,0:T(8,128)(2,1)S(1)}, u32[]{:S(2)}, u32[]{:S(2)}) collective-permute-start(bf16[512,512]{1,0:T(8,128)(2,1)S(1)} %shard_map.42.refs_0_), channel_id=1, source_target_pairs={{0,128},{1,385},{2,130},{3,387},{4,132},{5,389},{6,134},{7,391},{8... | collective-permute-start | bytes 1572872 | tf_op jit(solution)/shard_map/ppermute | solution.py:267
  18.5 0.0 collective-permute-done.1.refs_1_
  18.5 3.2 %collective-permute-start.2 = (bf16[256,512]{1,0:T(8,128)(2,1)S(1)}, bf16[256,512]{1,0:T(8,128)(2,1)S(1)}, u32[]{:S(2)}, u32[]{:S(2)}) collective-permute-start(bf16[256,512]{1,0:T(8,128)(2,1)S(1)} %collective-permute-done.1.refs_1_), channel_id=1, source_target_pairs={{0,32},{32,0},{64,96},{96,64},{128,160},{160,128},{192,224},{224,1... | collective-permute-start | bytes 786440 | tf_op jit(solution)/shard_map/ppermute | solution.py:272
  21.7 1.2 %shard_map.43 = (s32[16,256]{1,0:T(8,128)S(1)}, s32[256,128]{1,0:T(8,128)S(1)}) custom-call(s32[1024,128]{1,0:T(8,128)} %bitcast.1), custom_call_target="tpu_custom_call" | custom-call | tf_op jit(solution)/shard_map/pallas_call | solution.py:94
  22.9 5.9 %collective-permute-start.7 = (bf16[256,512]{1,0:T(8,128)(2,1)S(1)}, bf16[256,512]{1,0:T(8,128)(2,1)S(1)}, u32[]{:S(2)}, u32[]{:S(2)}) collective-permute-start(bf16[256,512]{1,0:T(8,128)(2,1)S(1)} %collective-permute-done.1.refs_1_), channel_id=1, source_target_pairs={{0,384},{1,129},{2,386},{3,131},{4,388},{5,133},{6,390},{7,135},{8... | collective-permute-start | bytes 786440 | tf_op jit(solution)/shard_map/ppermute | solution.py:267
  28.8 0.0 collective-permute-done.2.refs_2_
  28.8 5.0 %collective-permute-start.8 = (bf16[256,512]{1,0:T(8,128)(2,1)S(1)}, bf16[256,512]{1,0:T(8,128)(2,1)S(1)}, u32[]{:S(2)}, u32[]{:S(2)}) collective-permute-start(bf16[256,512]{1,0:T(8,128)(2,1)S(1)} %collective-permute-done.2.refs_2_), channel_id=1, source_target_pairs={{0,384},{1,129},{2,386},{3,131},{4,388},{5,133},{6,390},{7,135},{8... | collective-permute-start | bytes 786440 | tf_op jit(solution)/shard_map/ppermute | solution.py:267
  33.8 3.2 %collective-permute-start.5 = (bf16[256,512]{1,0:T(8,128)(2,1)S(1)}, bf16[256,512]{1,0:T(8,128)(2,1)S(1)}, u32[]{:S(2)}, u32[]{:S(2)}) collective-permute-start(bf16[256,512]{1,0:T(8,128)(2,1)S(1)} %collective-permute-done.1.refs_1_), channel_id=1, source_target_pairs={{0,128},{1,385},{2,130},{3,387},{4,132},{5,389},{6,134},{7,391},{8... | collective-permute-start | bytes 786440 | tf_op jit(solution)/shard_map/ppermute | solution.py:267
  37.0 0.0 collective-permute-done.4.refs_4_
  37.0 3.4 %collective-permute-start.6 = (bf16[256,512]{1,0:T(8,128)(2,1)S(1)}, bf16[256,512]{1,0:T(8,128)(2,1)S(1)}, u32[]{:S(2)}, u32[]{:S(2)}) collective-permute-start(bf16[256,512]{1,0:T(8,128)(2,1)S(1)} %collective-permute-done.2.refs_2_), channel_id=1, source_target_pairs={{0,128},{1,385},{2,130},{3,387},{4,132},{5,389},{6,134},{7,391},{8... | collective-permute-start | bytes 786440 | tf_op jit(solution)/shard_map/ppermute | solution.py:267
  40.4 0.0 collective-permute-done.3.refs_3_
  40.4 2.5 %collective-permute-start.9 = (bf16[512,512]{1,0:T(8,128)(2,1)S(1)}, bf16[512,512]{1,0:T(8,128)(2,1)S(1)}, u32[]{:S(2)}, u32[]{:S(2)}) collective-permute-start(bf16[512,512]{1,0:T(8,128)(2,1)S(1)} %collective-permute-done.3.refs_3_), channel_id=1, source_target_pairs={{0,128},{1,385},{2,130},{3,387},{4,132},{5,389},{6,134},{7,391},{8... | collective-permute-start | bytes 1572872 | tf_op jit(solution)/shard_map/ppermute | solution.py:267
  42.9 1.2 %shard_map.44 = (f32[24,256]{1,0:T(8,128)S(1)}, bf16[1024,512]{1,0:T(8,128)(2,1)}) custom-call(bf16[512,512]{1,0:T(8,128)(2,1)S(1)} %shard_map.42.refs_0_, bf16[256,512]{1,0:T(8,128)(2,1)S(1)} %collective-permute-done.1.refs_1_, bf16[256,512]{1,0:T(8,128)(2,1)S(1)} %collective-permute-done.2.refs_2_, ...), custom_call_target="tpu_custom_call" | custom-call | flops 671088640 | bytes 1048576 | tf_op jit(solution)/shard_map/pallas_call | solution.py:181
  44.1 0.0 collective-permute-done.7.refs_7_.first_ref
  44.1 0.0 collective-permute-done.8.refs_8_.second_ref
  44.1 3.0 %collective-permute-start.10 = (bf16[512,512]{1,0:T(8,128)(2,1)S(1)}, bf16[512,512]{1,0:T(8,128)(2,1)S(1)}, u32[]{:S(2)}, u32[]{:S(2)}) collective-permute-start(bf16[512,512]{1,0:T(8,128)(2,1)S(1)} %shard_map.48), channel_id=1, source_target_pairs={{0,384},{1,129},{2,386},{3,131},{4,388},{5,133},{6,390},{7,135},{8... | collective-permute-start | bytes 1572872 | tf_op jit(solution)/shard_map/ppermute | solution.py:267
  47.2 2.5 %shard_map.45 = (f32[24,256]{1,0:T(8,128)S(1)}, bf16[1024,512]{1,0:T(8,128)(2,1)}) custom-call(bf16[512,512]{1,0:T(8,128)(2,1)S(1)} %shard_map.42.refs_0_, bf16[256,512]{1,0:T(8,128)(2,1)S(1)} %collective-permute-done.1.refs_1_, bf16[256,512]{1,0:T(8,128)(2,1)S(1)} %collective-permute-done.2.refs_2_, bf16[512,512]{1,0:T(8,128)(2,1)S(1)} %collective-permute-done.3.refs_3_, ...), custom_call_target="tpu_custom_call" | custom-call | flops 1744830464 | bytes 2097152 | tf_op jit(solution)/shard_map/pallas_call | solution.py:181
  49.6 0.0 collective-permute-done.5.refs_5_
  49.6 0.0 collective-permute-done.6.refs_6_
  49.7 4.1 %shard_map.46 = (f32[24,256]{1,0:T(8,128)S(1)}, bf16[1024,512]{1,0:T(8,128)(2,1)}) custom-call(bf16[512,512]{1,0:T(8,128)(2,1)S(1)} %shard_map.42.refs_0_, bf16[256,512]{1,0:T(8,128)(2,1)S(1)} %collective-permute-done.1.refs_1_, bf16[256,512]{1,0:T(8,128)(2,1)S(1)} %collective-permute-done.2.refs_2_, bf16[512,512]{1,0:T(8,128)(2,1)S(1)} %collective-permute-done.3.refs_3_, ...), custom_call_target="tpu_custom_call" | custom-call | flops 2818572288 | bytes 3145728 | tf_op jit(solution)/shard_map/pallas_call | solution.py:181
  53.7 0.0 collective-permute-done.9.refs_9_
  53.7 2.3 %shard_map.47 = (f32[24,256]{1,0:T(8,128)S(1)}, bf16[512,512]{1,0:T(8,128)(2,1)}) custom-call(bf16[512,512]{1,0:T(8,128)(2,1)S(1)} %shard_map.42.refs_0_, bf16[256,512]{1,0:T(8,128)(2,1)S(1)} %collective-permute-done.1.refs_1_, bf16[256,512]{1,0:T(8,128)(2,1)S(1)} %collective-permute-done.2.refs_2_, bf16[512,512]{1,0:T(8,128)(2,1)S(1)} %collective-permute-done.3.refs_3_, ...), custom_call_target="tpu_custom_call" | custom-call | flops 1811939328 | bytes 3670016 | tf_op jit(solution)/shard_map/pallas_call | solution.py:181
  56.1 4.5 %collective-permute-done.10.refs_10_ = bf16[512,512]{1,0:T(8,128)(2,1)S(1)} collective-permute-done((bf16[512,512]{1,0:T(8,128)(2,1)S(1)}, bf16[512,512]{1,0:T(8,128)(2,1)S(1)}, u32[]{:S(2)}, u32[]{:S(2)}) %collective-permute-start.10) | collective-permute-done | bytes 524320 | tf_op jit(solution)/shard_map/ppermute | solution.py:267
  60.6 0.0 copy-start.1
  60.6 3.2 %shard_map.49 = (f32[24,256]{1,0:T(8,128)S(1)}, bf16[512,512]{1,0:T(8,128)(2,1)}, f32[32,1,128]{2,1,0:T(1,128)}) custom-call(bf16[512,512]{1,0:T(8,128)(2,1)S(1)} %shard_map.42.refs_0_, bf16[256,512]{1,0:T(8,128)(2,1)S(1)} %collective-permute-done.1.refs_1_, bf16[256,512]{1,0:T(8,128)(2,1)S(1)} %collective-permute-done.2.refs_2_, ...), custom_call_target="tpu_custom_call" | custom-call | flops 2080374784 | bytes 4194304 | tf_op jit(solution)/shard_map/pallas_call | solution.py:181
  63.8 19.5 %all-to-all-start = ((f32[32,1,128]{2,1,0:T(1,128)}), f32[32,1,128]{2,1,0:T(1,128)S(1)}, u32[]{:S(2)}, u32[]{:S(2)}) async-start(f32[32,1,128]{2,1,0:T(1,128)} %get-tuple-element.37), calls=%async_computation | async-start | bytes 32768 | tf_op jit(solution)/shard_map/all_to_all | solution.py:321
  83.4 0.0 copy-done.1
  83.4 6.1 %shard_map.50 = f32[256,512]{1,0:T(8,128)} custom-call(bf16[1024,512]{1,0:T(8,128)(2,1)} %get-tuple-element.24.refs_0_, bf16[1024,512]{1,0:T(8,128)(2,1)} %get-tuple-element.28.refs_1_, bf16[1024,512]{1,0:T(8,128)(2,1)} %get-tuple-element.30.refs_2_, bf16[512,512]{1,0:T(8,128)(2,1)} %get-tuple-element.32.refs_3_, ...), custom_call_target="tpu_custom_call" | custom-call | flops 3221225472 | bytes 4194304 | tf_op jit(solution)/shard_map/pallas_call | solution.py:243
  89.5 8.1 %all-to-all-done = f32[32,1,128]{2,1,0:T(1,128)S(1)} async-done(((f32[32,1,128]{2,1,0:T(1,128)}), f32[32,1,128]{2,1,0:T(1,128)S(1)}, u32[]{:S(2)}, u32[]{:S(2)}) %all-to-all-start) | async-done | bytes 16416 | tf_op jit(solution)/shard_map/all_to_all | solution.py:321
  97.5 0.6 reduce_sum.9
  (2 shorter events, 0.1 us)
Async XLA Ops:
  0.6 1.0 %copy-start = (f32[256,512]{1,0:T(8,128)S(1)}, f32[256,512]{1,0:T(8,128)}, u32[]{:S(2)}) copy-start(f32[256,512]{1,0:T(8,128)} %refs_7_.1) | copy-start | bytes 1572868
  1.8 9.3 %collective-permute-start = (bf16[256,512]{1,0:T(8,128)(2,1)S(1)}, bf16[256,512]{1,0:T(8,128)(2,1)S(1)}, u32[]{:S(2)}, u32[]{:S(2)}) collective-permute-start(bf16[256,512]{1,0:T(8,128)(2,1)S(1)} %shard_map.41.first_ref), channel_id=1, source_target_pairs={{0,32},{32,0},{64,96},{96,64},{128,160},{160,128},{192,224},{224,1... | collective-permute-start | bytes 786440 | tf_op jit(solution)/shard_map/ppermute | solution.py:272
  6.2 12.3 %collective-permute-start.1 = (bf16[256,512]{1,0:T(8,128)(2,1)S(1)}, bf16[256,512]{1,0:T(8,128)(2,1)S(1)}, u32[]{:S(2)}, u32[]{:S(2)}) collective-permute-start(bf16[256,512]{1,0:T(8,128)(2,1)S(1)} %shard_map.41.first_ref), channel_id=1, source_target_pairs={{0,64},{32,96},{64,0},{96,32},{128,192},{160,224},{192,128},{224,1... | collective-permute-start | bytes 786440 | tf_op jit(solution)/shard_map/ppermute | solution.py:272
  11.2 25.8 %collective-permute-start.4 = (bf16[512,512]{1,0:T(8,128)(2,1)S(1)}, bf16[512,512]{1,0:T(8,128)(2,1)S(1)}, u32[]{:S(2)}, u32[]{:S(2)}) collective-permute-start(bf16[512,512]{1,0:T(8,128)(2,1)S(1)} %shard_map.42.refs_0_), channel_id=1, source_target_pairs={{0,384},{1,129},{2,386},{3,131},{4,388},{5,133},{6,390},{7,135},{8... | collective-permute-start | bytes 1572872 | tf_op jit(solution)/shard_map/ppermute | solution.py:267
  15.3 25.1 %collective-permute-start.3 = (bf16[512,512]{1,0:T(8,128)(2,1)S(1)}, bf16[512,512]{1,0:T(8,128)(2,1)S(1)}, u32[]{:S(2)}, u32[]{:S(2)}) collective-permute-start(bf16[512,512]{1,0:T(8,128)(2,1)S(1)} %shard_map.42.refs_0_), channel_id=1, source_target_pairs={{0,128},{1,385},{2,130},{3,387},{4,132},{5,389},{6,134},{7,391},{8... | collective-permute-start | bytes 1572872 | tf_op jit(solution)/shard_map/ppermute | solution.py:267
  18.5 10.3 %collective-permute-start.2 = (bf16[256,512]{1,0:T(8,128)(2,1)S(1)}, bf16[256,512]{1,0:T(8,128)(2,1)S(1)}, u32[]{:S(2)}, u32[]{:S(2)}) collective-permute-start(bf16[256,512]{1,0:T(8,128)(2,1)S(1)} %collective-permute-done.1.refs_1_), channel_id=1, source_target_pairs={{0,32},{32,0},{64,96},{96,64},{128,160},{160,128},{192,224},{224,1... | collective-permute-start | bytes 786440 | tf_op jit(solution)/shard_map/ppermute | solution.py:272
  22.9 21.2 %collective-permute-start.7 = (bf16[256,512]{1,0:T(8,128)(2,1)S(1)}, bf16[256,512]{1,0:T(8,128)(2,1)S(1)}, u32[]{:S(2)}, u32[]{:S(2)}) collective-permute-start(bf16[256,512]{1,0:T(8,128)(2,1)S(1)} %collective-permute-done.1.refs_1_), channel_id=1, source_target_pairs={{0,384},{1,129},{2,386},{3,131},{4,388},{5,133},{6,390},{7,135},{8... | collective-permute-start | bytes 786440 | tf_op jit(solution)/shard_map/ppermute | solution.py:267
  28.8 15.3 %collective-permute-start.8 = (bf16[256,512]{1,0:T(8,128)(2,1)S(1)}, bf16[256,512]{1,0:T(8,128)(2,1)S(1)}, u32[]{:S(2)}, u32[]{:S(2)}) collective-permute-start(bf16[256,512]{1,0:T(8,128)(2,1)S(1)} %collective-permute-done.2.refs_2_), channel_id=1, source_target_pairs={{0,384},{1,129},{2,386},{3,131},{4,388},{5,133},{6,390},{7,135},{8... | collective-permute-start | bytes 786440 | tf_op jit(solution)/shard_map/ppermute | solution.py:267
  33.8 15.8 %collective-permute-start.5 = (bf16[256,512]{1,0:T(8,128)(2,1)S(1)}, bf16[256,512]{1,0:T(8,128)(2,1)S(1)}, u32[]{:S(2)}, u32[]{:S(2)}) collective-permute-start(bf16[256,512]{1,0:T(8,128)(2,1)S(1)} %collective-permute-done.1.refs_1_), channel_id=1, source_target_pairs={{0,128},{1,385},{2,130},{3,387},{4,132},{5,389},{6,134},{7,391},{8... | collective-permute-start | bytes 786440 | tf_op jit(solution)/shard_map/ppermute | solution.py:267
  37.0 12.6 %collective-permute-start.6 = (bf16[256,512]{1,0:T(8,128)(2,1)S(1)}, bf16[256,512]{1,0:T(8,128)(2,1)S(1)}, u32[]{:S(2)}, u32[]{:S(2)}) collective-permute-start(bf16[256,512]{1,0:T(8,128)(2,1)S(1)} %collective-permute-done.2.refs_2_), channel_id=1, source_target_pairs={{0,128},{1,385},{2,130},{3,387},{4,132},{5,389},{6,134},{7,391},{8... | collective-permute-start | bytes 786440 | tf_op jit(solution)/shard_map/ppermute | solution.py:267
  40.4 13.3 %collective-permute-start.9 = (bf16[512,512]{1,0:T(8,128)(2,1)S(1)}, bf16[512,512]{1,0:T(8,128)(2,1)S(1)}, u32[]{:S(2)}, u32[]{:S(2)}) collective-permute-start(bf16[512,512]{1,0:T(8,128)(2,1)S(1)} %collective-permute-done.3.refs_3_), channel_id=1, source_target_pairs={{0,128},{1,385},{2,130},{3,387},{4,132},{5,389},{6,134},{7,391},{8... | collective-permute-start | bytes 1572872 | tf_op jit(solution)/shard_map/ppermute | solution.py:267
  44.1 16.5 %collective-permute-start.10 = (bf16[512,512]{1,0:T(8,128)(2,1)S(1)}, bf16[512,512]{1,0:T(8,128)(2,1)S(1)}, u32[]{:S(2)}, u32[]{:S(2)}) collective-permute-start(bf16[512,512]{1,0:T(8,128)(2,1)S(1)} %shard_map.48), channel_id=1, source_target_pairs={{0,384},{1,129},{2,386},{3,131},{4,388},{5,133},{6,390},{7,135},{8... | collective-permute-start | bytes 1572872 | tf_op jit(solution)/shard_map/ppermute | solution.py:267
  60.6 22.8 %copy-start.1 = (f32[256,512]{1,0:T(8,128)S(1)}, f32[256,512]{1,0:T(8,128)}, u32[]{:S(2)}) copy-start(f32[256,512]{1,0:T(8,128)} %refs_7_.1) | copy-start | bytes 1572868
  63.8 33.7 %all-to-all-start = ((f32[32,1,128]{2,1,0:T(1,128)}), f32[32,1,128]{2,1,0:T(1,128)S(1)}, u32[]{:S(2)}, u32[]{:S(2)}) async-start(f32[32,1,128]{2,1,0:T(1,128)} %get-tuple-element.37), calls=%async_computation | async-start | bytes 32768 | tf_op jit(solution)/shard_map/all_to_all | solution.py:321

commit v3 on v2

--- a/solution.py
+++ b/solution.py
@@ -130,35 +130,31 @@
 
     sums = [jnp.zeros((8, B), jnp.float32)] * last
     hits = jnp.zeros((8, B), jnp.float32)
-    row_sums = {}
-    for pair in range(first, last, 2):
-        both = jnp.concatenate([blocks[pair], blocks[pair + 1]], axis=0)
-        both_rows = lax.broadcasted_iota(jnp.int32, (2 * B, B), 0)
-        both_total = jnp.zeros((2 * B, 128), jnp.float32)
-        for c in range(first):
-            raw = nt_dot(both, blocks[c])
-            e = jnp.exp2(raw * SCALE)
-            both_total = both_total + (e[:, :128] + e[:, 128:])
-            sums[c] = sums[c] + fold(e)
-            found = jnp.where(both_rows == place[c : c + 1, :] - pair * B, raw, 0.0)
-            hits = hits + 2.0 * fold(found)
-        for a in (pair, pair + 1):
-            total = both_total[(a - pair) * B : (a - pair + 1) * B, :]
-            for c in range(a, last):
-                raw = nt_dot(blocks[a], blocks[c])
-                e = jnp.exp2(raw * SCALE)
-                if c == a:
-                    e = jnp.where(rows == lanes, 0.0, e)
-                total = total + (e[:, :128] + e[:, 128:])
-                found = fold(jnp.where(rows == place[c : c + 1, :] - a * B, raw, 0.0))
-                if c != a:
-                    sums[c] = sums[c] + fold(e)
-                    found = 2.0 * found
-                hits = hits + found
-            row_sums[a] = jnp.sum(total.T, axis=0, keepdims=True)
+    new = jnp.concatenate(blocks[first:], axis=0)
+    new_rows = lax.broadcasted_iota(jnp.int32, (new.shape[0], B), 0) + first * B
+    row_sums = [jnp.zeros((B, 128), jnp.float32)] * (last - first)
+    for c in range(last):
+        count = last - first if c < first else c - first + 1
+        raw = nt_dot(new[: count * B, :], blocks[c])
+        found = jnp.where(new_rows[: count * B, :] == place[c : c + 1, :], raw, 0.0)
+        e = jnp.exp2(raw * SCALE)
+        if c >= first:
+            count -= 1
+            own = jnp.where(rows == lanes, 0.0, e[count * B :, :])
+            row_sums[count] = row_sums[count] + (own[:, :128] + own[:, 128:])
+            hits = hits + fold(found[count * B :, :])
+        if count > 0:
+            sums[c] = fold(e[: count * B, :])
+            hits = hits + 2.0 * fold(found[: count * B, :])
+        for k in range(count):
+            part = e[k * B : (k + 1) * B, :]
+            row_sums[k] = row_sums[k] + (part[:, :128] + part[:, 128:])
     for s in range(last):
         total = jnp.sum(sums[s], axis=0, keepdims=True)
-        total = total + (sums_in[s : s + 1, :] if s < first else row_sums[s])
+        if s < first:
+            total = total + sums_in[s : s + 1, :]
+        else:
+            total = total + jnp.sum(row_sums[s - first].T, axis=0, keepdims=True)
         sums_out[s : s + 1, :] = total
     if last < SLOTS:
         sums_out[last:SLOTS, :] = jnp.zeros((SLOTS - last, B), jnp.float32)
@@ -310,9 +306,11 @@
         old.extend(new)
         return (part_sums,), rest
 
-    near_1, near_3 = lax.optimization_barrier((near_1, near_3))
+    near_1, near_3, z2_1 = lax.optimization_barrier((near_1, near_3, z2_1))
     near_2 = shift_x(near_1, 1)
-    far_2 = shift_x(stack(z2_3, z3_3), 3)
+    far_pair = stack(z2_3, z3_3)
+    far_pair, near = lax.optimization_barrier((far_pair, near))
+    far_2 = shift_x(far_pair, 3)
     state, _ = add(near, z2, z3)
     state, _ = add(near_1, near_3)
     state, _ = add(z2_1, z3_1, z2_3, z3_3)

time: 100 us -> 98 us (0.980)
  starting transfers between devices: 62.2 us -> 59.2 us
    ppermute x8, starting transfers between devices: 30.2 us -> 28.2 us  [shift_x(): return lax.ppermute(value, ('group', 'dp'), perm)]
  transfers between devices with their start and end apart: 12 -> 12, of which waited for: 2 -> 2; matrix products, arithmetic and copies ran while one was open for 0% -> 0% of each run, Pallas kernels for 17% -> 18%
where the time goes in v3:
time: 98 us; the launch traced here: 97.4 us
  starting transfers between devices  59.2 us (60%)
  Pallas kernels  20.6 us (21%)
  waiting for transfers between devices  13.3 us (14%)
  between operations  2.68 us (3%)
  local copies, waits for them, and re-layouts  1.04 us (1%)
    ppermute x8, starting transfers between devices, shift_x(): return lax.ppermute(value, ('group', 'dp'), perm)  28.2 us
    all_to_all x1, starting transfers between devices, on_device(): losses = lax.all_to_all(part, 'dp', 0, 0)  18.6 us
    pallas_call x5, Pallas kernels, sums(): pl.pallas_call(functools.partial(sums_kernel, first, last, len(old) + len...  13.1 us
    ppermute x3, starting transfers between devices, swap_z(): return lax.ppermute(value, 'group', perm)  12.4 us
    all_to_all x1, waiting for transfers between devices, on_device(): losses = lax.all_to_all(part, 'dp', 0, 0)  8.09 us
    pallas_call x1, Pallas kernels, grads(): pl.pallas_call(grad_kernel, out_shape=jax.ShapeDtypeStruct((B, E), jnp.fl...  6.06 us
    ppermute x8, waiting for transfers between devices, shift_x(): return lax.ppermute(value, ('group', 'dp'), perm)  5.15 us
  transfers between devices with their start and end apart: 12, of which 2 were waited for; matrix products, arithmetic and copies ran while one was open for 0% of the time, Pallas kernels for 18%

profile of v3, /device:TPU:1, one launch (start us, length us, event | category | flops | bytes accessed | tf_op | source)
XLA Modules:
  0.0 97.4 jit_solution(4329486782037078328)
XLA Ops:
  0.6 0.0 copy-start
  0.6 1.0 %copy-done = f32[256,512]{1,0:T(8,128)S(1)} copy-done((f32[256,512]{1,0:T(8,128)S(1)}, f32[256,512]{1,0:T(8,128)}, u32[]{:S(2)}) %copy-start) | copy-done | bytes 524312
  1.7 0.1 shard_map.41.first_ref
  1.8 4.4 %collective-permute-start.4 = (bf16[256,512]{1,0:T(8,128)(2,1)S(1)}, bf16[256,512]{1,0:T(8,128)(2,1)S(1)}, u32[]{:S(2)}, u32[]{:S(2)}) collective-permute-start(bf16[256,512]{1,0:T(8,128)(2,1)S(1)} %shard_map.41.first_ref), channel_id=1, source_target_pairs={{0,32},{32,0},{64,96},{96,64},{128,160},{160,128},{192,224},{224,1... | collective-permute-start | bytes 786440 | tf_op jit(solution)/shard_map/ppermute | solution.py:268
  6.2 4.9 %collective-permute-start = (bf16[256,512]{1,0:T(8,128)(2,1)S(1)}, bf16[256,512]{1,0:T(8,128)(2,1)S(1)}, u32[]{:S(2)}, u32[]{:S(2)}) collective-permute-start(bf16[256,512]{1,0:T(8,128)(2,1)S(1)} %shard_map.41.first_ref), channel_id=1, source_target_pairs={{0,64},{32,96},{64,0},{96,32},{128,192},{160,224},{192,128},{224,1... | collective-permute-start | bytes 786440 | tf_op jit(solution)/shard_map/ppermute | solution.py:268
  11.1 0.0 collective-permute-done.4.second_ref
  11.2 4.1 %collective-permute-start.6 = (bf16[512,512]{1,0:T(8,128)(2,1)S(1)}, bf16[512,512]{1,0:T(8,128)(2,1)S(1)}, u32[]{:S(2)}, u32[]{:S(2)}) collective-permute-start(bf16[512,512]{1,0:T(8,128)(2,1)S(1)} %shard_map.44.refs_0_), channel_id=1, source_target_pairs={{0,384},{1,129},{2,386},{3,131},{4,388},{5,133},{6,390},{7,135},{8... | collective-permute-start | bytes 1572872 | tf_op jit(solution)/shard_map/ppermute | solution.py:263
  15.3 3.2 %collective-permute-start.5 = (bf16[512,512]{1,0:T(8,128)(2,1)S(1)}, bf16[512,512]{1,0:T(8,128)(2,1)S(1)}, u32[]{:S(2)}, u32[]{:S(2)}) collective-permute-start(bf16[512,512]{1,0:T(8,128)(2,1)S(1)} %shard_map.44.refs_0_), channel_id=1, source_target_pairs={{0,128},{1,385},{2,130},{3,387},{4,132},{5,389},{6,134},{7,391},{8... | collective-permute-start | bytes 1572872 | tf_op jit(solution)/shard_map/ppermute | solution.py:263
  18.5 0.0 collective-permute-done.refs_1_
  18.5 3.2 %collective-permute-start.2 = (bf16[256,512]{1,0:T(8,128)(2,1)S(1)}, bf16[256,512]{1,0:T(8,128)(2,1)S(1)}, u32[]{:S(2)}, u32[]{:S(2)}) collective-permute-start(bf16[256,512]{1,0:T(8,128)(2,1)S(1)} %collective-permute-done.refs_1_), channel_id=1, source_target_pairs={{0,32},{32,0},{64,96},{96,64},{128,160},{160,128},{192,224},{224,1... | collective-permute-start | bytes 786440 | tf_op jit(solution)/shard_map/ppermute | solution.py:268
  21.7 7.2 %collective-permute-start.7 = (bf16[256,512]{1,0:T(8,128)(2,1)S(1)}, bf16[256,512]{1,0:T(8,128)(2,1)S(1)}, u32[]{:S(2)}, u32[]{:S(2)}) collective-permute-start(bf16[256,512]{1,0:T(8,128)(2,1)S(1)} %collective-permute-done.refs_1_), channel_id=1, source_target_pairs={{0,128},{1,385},{2,130},{3,387},{4,132},{5,389},{6,134},{7,391},{8... | collective-permute-start | bytes 786440 | tf_op jit(solution)/shard_map/ppermute | solution.py:263
  28.8 1.2 %shard_map.42 = (s32[16,256]{1,0:T(8,128)S(1)}, s32[256,128]{1,0:T(8,128)S(1)}) custom-call(s32[1024,128]{1,0:T(8,128)} %bitcast.1), custom_call_target="tpu_custom_call" | custom-call | tf_op jit(solution)/shard_map/pallas_call | solution.py:94
  30.1 1.9 %collective-permute-start.1 = (bf16[256,512]{1,0:T(8,128)(2,1)S(1)}, bf16[256,512]{1,0:T(8,128)(2,1)S(1)}, u32[]{:S(2)}, u32[]{:S(2)}) collective-permute-start(bf16[256,512]{1,0:T(8,128)(2,1)S(1)} %collective-permute-done.refs_1_), channel_id=1, source_target_pairs={{0,384},{1,129},{2,386},{3,131},{4,388},{5,133},{6,390},{7,135},{8... | collective-permute-start | bytes 786440 | tf_op jit(solution)/shard_map/ppermute | solution.py:263
  32.0 0.0 collective-permute-done.2.refs_2_
  32.0 2.1 %collective-permute-start.3 = (bf16[256,512]{1,0:T(8,128)(2,1)S(1)}, bf16[256,512]{1,0:T(8,128)(2,1)S(1)}, u32[]{:S(2)}, u32[]{:S(2)}) collective-permute-start(bf16[256,512]{1,0:T(8,128)(2,1)S(1)} %collective-permute-done.2.refs_2_), channel_id=1, source_target_pairs={{0,384},{1,129},{2,386},{3,131},{4,388},{5,133},{6,390},{7,135},{8... | collective-permute-start | bytes 786440 | tf_op jit(solution)/shard_map/ppermute | solution.py:263
  34.1 0.0 collective-permute-done.7.refs_5_
  34.1 4.4 %collective-permute-start.8 = (bf16[256,512]{1,0:T(8,128)(2,1)S(1)}, bf16[256,512]{1,0:T(8,128)(2,1)S(1)}, u32[]{:S(2)}, u32[]{:S(2)}) collective-permute-start(bf16[256,512]{1,0:T(8,128)(2,1)S(1)} %collective-permute-done.2.refs_2_), channel_id=1, source_target_pairs={{0,128},{1,385},{2,130},{3,387},{4,132},{5,389},{6,134},{7,391},{8... | collective-permute-start | bytes 786440 | tf_op jit(solution)/shard_map/ppermute | solution.py:263
  38.5 0.0 collective-permute-done.6.refs_4_
  38.5 0.0 collective-permute-done.5.refs_3_
  38.5 3.4 %collective-permute-start.9 = (bf16[512,512]{1,0:T(8,128)(2,1)S(1)}, bf16[512,512]{1,0:T(8,128)(2,1)S(1)}, u32[]{:S(2)}, u32[]{:S(2)}) collective-permute-start(bf16[512,512]{1,0:T(8,128)(2,1)S(1)} %collective-permute-done.5.refs_3_), channel_id=1, source_target_pairs={{0,128},{1,385},{2,130},{3,387},{4,132},{5,389},{6,134},{7,391},{8... | collective-permute-start | bytes 1572872 | tf_op jit(solution)/shard_map/ppermute | solution.py:263
  41.9 0.0 collective-permute-done.1.first_ref.refs_7_
  41.9 0.0 collective-permute-done.3.second_ref.refs_8_
  42.0 1.9 %collective-permute-start.10 = (bf16[512,512]{1,0:T(8,128)(2,1)S(1)}, bf16[512,512]{1,0:T(8,128)(2,1)S(1)}, u32[]{:S(2)}, u32[]{:S(2)}) collective-permute-start(bf16[512,512]{1,0:T(8,128)(2,1)S(1)} %shard_map.43), channel_id=1, source_target_pairs={{0,384},{1,129},{2,386},{3,131},{4,388},{5,133},{6,390},{7,135},{8... | collective-permute-start | bytes 1572872 | tf_op jit(solution)/shard_map/ppermute | solution.py:263
  43.9 1.4 %shard_map.45 = (f32[24,256]{1,0:T(8,128)S(1)}, bf16[1024,512]{1,0:T(8,128)(2,1)}) custom-call(bf16[512,512]{1,0:T(8,128)(2,1)S(1)} %shard_map.44.refs_0_, bf16[256,512]{1,0:T(8,128)(2,1)S(1)} %collective-permute-done.refs_1_, bf16[256,512]{1,0:T(8,128)(2,1)S(1)} %collective-permute-done.2.refs_2_, ...), custom_call_target="tpu_custom_call" | custom-call | flops 671088640 | bytes 1048576 | tf_op jit(solution)/shard_map/pallas_call | solution.py:177
  45.4 2.5 %shard_map.46 = (f32[24,256]{1,0:T(8,128)S(1)}, bf16[1024,512]{1,0:T(8,128)(2,1)}) custom-call(bf16[512,512]{1,0:T(8,128)(2,1)S(1)} %shard_map.44.refs_0_, bf16[256,512]{1,0:T(8,128)(2,1)S(1)} %collective-permute-done.refs_1_, bf16[256,512]{1,0:T(8,128)(2,1)S(1)} %collective-permute-done.2.refs_2_, bf16[512,512]{1,0:T(8,128)(2,1)S(1)} %collective-permute-done.5.refs_3_, ...), custom_call_target="tpu_custom_call" | custom-call | flops 1744830464 | bytes 2097152 | tf_op jit(solution)/shard_map/pallas_call | solution.py:177
  47.8 0.0 collective-permute-done.8.refs_6_
  47.9 3.7 %shard_map.47 = (f32[24,256]{1,0:T(8,128)S(1)}, bf16[1024,512]{1,0:T(8,128)(2,1)}) custom-call(bf16[512,512]{1,0:T(8,128)(2,1)S(1)} %shard_map.44.refs_0_, bf16[256,512]{1,0:T(8,128)(2,1)S(1)} %collective-permute-done.refs_1_, bf16[256,512]{1,0:T(8,128)(2,1)S(1)} %collective-permute-done.2.refs_2_, bf16[512,512]{1,0:T(8,128)(2,1)S(1)} %collective-permute-done.5.refs_3_, ...), custom_call_target="tpu_custom_call" | custom-call | flops 2818572288 | bytes 3145728 | tf_op jit(solution)/shard_map/pallas_call | solution.py:177
  51.5 0.0 collective-permute-done.9.refs_9_
  51.6 2.3 %shard_map.48 = (f32[24,256]{1,0:T(8,128)S(1)}, bf16[512,512]{1,0:T(8,128)(2,1)}) custom-call(bf16[512,512]{1,0:T(8,128)(2,1)S(1)} %shard_map.44.refs_0_, bf16[256,512]{1,0:T(8,128)(2,1)S(1)} %collective-permute-done.refs_1_, bf16[256,512]{1,0:T(8,128)(2,1)S(1)} %collective-permute-done.2.refs_2_, bf16[512,512]{1,0:T(8,128)(2,1)S(1)} %collective-permute-done.5.refs_3_, ...), custom_call_target="tpu_custom_call" | custom-call | flops 1811939328 | bytes 3670016 | tf_op jit(solution)/shard_map/pallas_call | solution.py:177
  53.9 5.1 %collective-permute-done.10.refs_10_ = bf16[512,512]{1,0:T(8,128)(2,1)S(1)} collective-permute-done((bf16[512,512]{1,0:T(8,128)(2,1)S(1)}, bf16[512,512]{1,0:T(8,128)(2,1)S(1)}, u32[]{:S(2)}, u32[]{:S(2)}) %collective-permute-start.10) | collective-permute-done | bytes 524320 | tf_op jit(solution)/shard_map/ppermute | solution.py:263
  59.0 0.0 copy-start.1
  59.0 3.2 %shard_map.49 = (f32[24,256]{1,0:T(8,128)S(1)}, bf16[512,512]{1,0:T(8,128)(2,1)}, f32[32,1,128]{2,1,0:T(1,128)}) custom-call(bf16[512,512]{1,0:T(8,128)(2,1)S(1)} %shard_map.44.refs_0_, bf16[256,512]{1,0:T(8,128)(2,1)S(1)} %collective-permute-done.refs_1_, bf16[256,512]{1,0:T(8,128)(2,1)S(1)} %collective-permute-done.2.refs_2_, ...), custom_call_target="tpu_custom_call" | custom-call | flops 2080374784 | bytes 4194304 | tf_op jit(solution)/shard_map/pallas_call | solution.py:177
  62.2 18.6 %all-to-all-start = ((f32[32,1,128]{2,1,0:T(1,128)}), f32[32,1,128]{2,1,0:T(1,128)S(1)}, u32[]{:S(2)}, u32[]{:S(2)}) async-start(f32[32,1,128]{2,1,0:T(1,128)} %get-tuple-element.43), calls=%async_computation | async-start | bytes 32768 | tf_op jit(solution)/shard_map/all_to_all | solution.py:319
  80.8 0.0 copy-done.1
  80.9 6.1 %shard_map.50 = f32[256,512]{1,0:T(8,128)} custom-call(bf16[1024,512]{1,0:T(8,128)(2,1)} %get-tuple-element.28.refs_0_, bf16[1024,512]{1,0:T(8,128)(2,1)} %get-tuple-element.32.refs_1_, bf16[1024,512]{1,0:T(8,128)(2,1)} %get-tuple-element.35.refs_2_, bf16[512,512]{1,0:T(8,128)(2,1)} %get-tuple-element.37.refs_3_, ...), custom_call_target="tpu_custom_call" | custom-call | flops 3221225472 | bytes 4194304 | tf_op jit(solution)/shard_map/pallas_call | solution.py:239
  86.9 8.1 %all-to-all-done = f32[32,1,128]{2,1,0:T(1,128)S(1)} async-done(((f32[32,1,128]{2,1,0:T(1,128)}), f32[32,1,128]{2,1,0:T(1,128)S(1)}, u32[]{:S(2)}, u32[]{:S(2)}) %all-to-all-start) | async-done | bytes 16416 | tf_op jit(solution)/shard_map/all_to_all | solution.py:319
  95.0 0.6 reduce_sum.9
  (2 shorter events, 0.1 us)
Async XLA Ops:
  0.6 1.0 %copy-start = (f32[256,512]{1,0:T(8,128)S(1)}, f32[256,512]{1,0:T(8,128)}, u32[]{:S(2)}) copy-start(f32[256,512]{1,0:T(8,128)} %refs_7_.1) | copy-start | bytes 1572868
  1.8 9.3 %collective-permute-start.4 = (bf16[256,512]{1,0:T(8,128)(2,1)S(1)}, bf16[256,512]{1,0:T(8,128)(2,1)S(1)}, u32[]{:S(2)}, u32[]{:S(2)}) collective-permute-start(bf16[256,512]{1,0:T(8,128)(2,1)S(1)} %shard_map.41.first_ref), channel_id=1, source_target_pairs={{0,32},{32,0},{64,96},{96,64},{128,160},{160,128},{192,224},{224,1... | collective-permute-start | bytes 786440 | tf_op jit(solution)/shard_map/ppermute | solution.py:268
  6.2 12.3 %collective-permute-start = (bf16[256,512]{1,0:T(8,128)(2,1)S(1)}, bf16[256,512]{1,0:T(8,128)(2,1)S(1)}, u32[]{:S(2)}, u32[]{:S(2)}) collective-permute-start(bf16[256,512]{1,0:T(8,128)(2,1)S(1)} %shard_map.41.first_ref), channel_id=1, source_target_pairs={{0,64},{32,96},{64,0},{96,32},{128,192},{160,224},{192,128},{224,1... | collective-permute-start | bytes 786440 | tf_op jit(solution)/shard_map/ppermute | solution.py:268
  11.2 27.3 %collective-permute-start.6 = (bf16[512,512]{1,0:T(8,128)(2,1)S(1)}, bf16[512,512]{1,0:T(8,128)(2,1)S(1)}, u32[]{:S(2)}, u32[]{:S(2)}) collective-permute-start(bf16[512,512]{1,0:T(8,128)(2,1)S(1)} %shard_map.44.refs_0_), channel_id=1, source_target_pairs={{0,384},{1,129},{2,386},{3,131},{4,388},{5,133},{6,390},{7,135},{8... | collective-permute-start | bytes 1572872 | tf_op jit(solution)/shard_map/ppermute | solution.py:263
  15.3 23.2 %collective-permute-start.5 = (bf16[512,512]{1,0:T(8,128)(2,1)S(1)}, bf16[512,512]{1,0:T(8,128)(2,1)S(1)}, u32[]{:S(2)}, u32[]{:S(2)}) collective-permute-start(bf16[512,512]{1,0:T(8,128)(2,1)S(1)} %shard_map.44.refs_0_), channel_id=1, source_target_pairs={{0,128},{1,385},{2,130},{3,387},{4,132},{5,389},{6,134},{7,391},{8... | collective-permute-start | bytes 1572872 | tf_op jit(solution)/shard_map/ppermute | solution.py:263
  18.5 13.5 %collective-permute-start.2 = (bf16[256,512]{1,0:T(8,128)(2,1)S(1)}, bf16[256,512]{1,0:T(8,128)(2,1)S(1)}, u32[]{:S(2)}, u32[]{:S(2)}) collective-permute-start(bf16[256,512]{1,0:T(8,128)(2,1)S(1)} %collective-permute-done.refs_1_), channel_id=1, source_target_pairs={{0,32},{32,0},{64,96},{96,64},{128,160},{160,128},{192,224},{224,1... | collective-permute-start | bytes 786440 | tf_op jit(solution)/shard_map/ppermute | solution.py:268
  21.7 12.5 %collective-permute-start.7 = (bf16[256,512]{1,0:T(8,128)(2,1)S(1)}, bf16[256,512]{1,0:T(8,128)(2,1)S(1)}, u32[]{:S(2)}, u32[]{:S(2)}) collective-permute-start(bf16[256,512]{1,0:T(8,128)(2,1)S(1)} %collective-permute-done.refs_1_), channel_id=1, source_target_pairs={{0,128},{1,385},{2,130},{3,387},{4,132},{5,389},{6,134},{7,391},{8... | collective-permute-start | bytes 786440 | tf_op jit(solution)/shard_map/ppermute | solution.py:263
  30.1 11.9 %collective-permute-start.1 = (bf16[256,512]{1,0:T(8,128)(2,1)S(1)}, bf16[256,512]{1,0:T(8,128)(2,1)S(1)}, u32[]{:S(2)}, u32[]{:S(2)}) collective-permute-start(bf16[256,512]{1,0:T(8,128)(2,1)S(1)} %collective-permute-done.refs_1_), channel_id=1, source_target_pairs={{0,384},{1,129},{2,386},{3,131},{4,388},{5,133},{6,390},{7,135},{8... | collective-permute-start | bytes 786440 | tf_op jit(solution)/shard_map/ppermute | solution.py:263
  32.0 9.9 %collective-permute-start.3 = (bf16[256,512]{1,0:T(8,128)(2,1)S(1)}, bf16[256,512]{1,0:T(8,128)(2,1)S(1)}, u32[]{:S(2)}, u32[]{:S(2)}) collective-permute-start(bf16[256,512]{1,0:T(8,128)(2,1)S(1)} %collective-permute-done.2.refs_2_), channel_id=1, source_target_pairs={{0,384},{1,129},{2,386},{3,131},{4,388},{5,133},{6,390},{7,135},{8... | collective-permute-start | bytes 786440 | tf_op jit(solution)/shard_map/ppermute | solution.py:263
  34.1 13.7 %collective-permute-start.8 = (bf16[256,512]{1,0:T(8,128)(2,1)S(1)}, bf16[256,512]{1,0:T(8,128)(2,1)S(1)}, u32[]{:S(2)}, u32[]{:S(2)}) collective-permute-start(bf16[256,512]{1,0:T(8,128)(2,1)S(1)} %collective-permute-done.2.refs_2_), channel_id=1, source_target_pairs={{0,128},{1,385},{2,130},{3,387},{4,132},{5,389},{6,134},{7,391},{8... | collective-permute-start | bytes 786440 | tf_op jit(solution)/shard_map/ppermute | solution.py:263
  38.5 13.0 %collective-permute-start.9 = (bf16[512,512]{1,0:T(8,128)(2,1)S(1)}, bf16[512,512]{1,0:T(8,128)(2,1)S(1)}, u32[]{:S(2)}, u32[]{:S(2)}) collective-permute-start(bf16[512,512]{1,0:T(8,128)(2,1)S(1)} %collective-permute-done.5.refs_3_), channel_id=1, source_target_pairs={{0,128},{1,385},{2,130},{3,387},{4,132},{5,389},{6,134},{7,391},{8... | collective-permute-start | bytes 1572872 | tf_op jit(solution)/shard_map/ppermute | solution.py:263
  42.0 17.0 %collective-permute-start.10 = (bf16[512,512]{1,0:T(8,128)(2,1)S(1)}, bf16[512,512]{1,0:T(8,128)(2,1)S(1)}, u32[]{:S(2)}, u32[]{:S(2)}) collective-permute-start(bf16[512,512]{1,0:T(8,128)(2,1)S(1)} %shard_map.43), channel_id=1, source_target_pairs={{0,384},{1,129},{2,386},{3,131},{4,388},{5,133},{6,390},{7,135},{8... | collective-permute-start | bytes 1572872 | tf_op jit(solution)/shard_map/ppermute | solution.py:263
  59.0 21.9 %copy-start.1 = (f32[256,512]{1,0:T(8,128)S(1)}, f32[256,512]{1,0:T(8,128)}, u32[]{:S(2)}) copy-start(f32[256,512]{1,0:T(8,128)} %refs_7_.1) | copy-start | bytes 1572868
  62.2 32.8 %all-to-all-start = ((f32[32,1,128]{2,1,0:T(1,128)}), f32[32,1,128]{2,1,0:T(1,128)S(1)}, u32[]{:S(2)}, u32[]{:S(2)}) async-start(f32[32,1,128]{2,1,0:T(1,128)} %get-tuple-element.43), calls=%async_computation | async-start | bytes 32768 | tf_op jit(solution)/shard_map/all_to_all | solution.py:319

commit v4 on v3

--- a/solution.py
+++ b/solution.py
@@ -22,7 +22,7 @@
     (2, 0), (2, 1),
     (2, 2), (2, 3),
 ]
-STAGES = (4, 8, 12, 14, 16)
+STAGES = (8, 12, 14, 16)
 CHUNK = 1024
 MIB = 1024 * 1024
 VMEM = pl.BlockSpec(memory_space=pltpu.VMEM)
@@ -289,11 +289,11 @@
     packed = pack(embeddings)
     place, own_place = places(partner, dp_count)
 
-    z1 = swap_z(packed, 1)
+    z1, place, own_place = lax.optimization_barrier((swap_z(packed, 1), place, own_place))
     z2 = swap_z(packed, 2)
     near = stack(packed, z1)
     near_1, near_3 = shift_x(near, 1), shift_x(near, 3)
-    z3, place, own_place = lax.optimization_barrier((swap_z(z2, 1), place, own_place))
+    z3 = swap_z(z2, 1)
     z2_1, z2_3 = shift_x(z2, 1), shift_x(z2, 3)
     z3_1, z3_3 = shift_x(z3, 1), shift_x(z3, 3)
 
@@ -311,8 +311,7 @@
     far_pair = stack(z2_3, z3_3)
     far_pair, near = lax.optimization_barrier((far_pair, near))
     far_2 = shift_x(far_pair, 3)
-    state, _ = add(near, z2, z3)
-    state, _ = add(near_1, near_3)
+    state, _ = add(near, z2, z3, near_1, near_3)
     state, _ = add(z2_1, z3_1, z2_3, z3_3)
     state, _ = add(near_2)
     (totals,), (part,) = add(far_2)

time: 98 us -> 98.9 us (level)
  waiting for transfers between devices: 13.3 us -> 14.5 us
    ppermute x8, waiting for transfers between devices: 5.15 us -> 6.4 us  [shift_x(): return lax.ppermute(value, ('group', 'dp'), perm)]
    pallas_call x5 -> x4, Pallas kernels: 13.1 us -> 13.2 us  [sums(): pl.pallas_call(functools.partial(sums_kernel, first, last, len(old) + len...]
  transfers between devices with their start and end apart: 12 -> 12, of which waited for: 2 -> 4; matrix products, arithmetic and copies ran while one was open for 0% -> 0% of each run, Pallas kernels for 18% -> 17%
where the time goes in v4:
time: 98.9 us; the launch traced here: 98.3 us
  starting transfers between devices  58.8 us (59%)
  Pallas kernels  20.7 us (21%)
  waiting for transfers between devices  14.5 us (15%)
  between operations  2.65 us (3%)
  local copies, waits for them, and re-layouts  1.04 us (1%)
    ppermute x8, starting transfers between devices, shift_x(): return lax.ppermute(value, ('group', 'dp'), perm)  27.2 us
    all_to_all x1, starting transfers between devices, on_device(): losses = lax.all_to_all(part, 'dp', 0, 0)  19.6 us
    pallas_call x4, Pallas kernels, sums(): pl.pallas_call(functools.partial(sums_kernel, first, last, len(old) + len...  13.2 us
    ppermute x3, starting transfers between devices, swap_z(): return lax.ppermute(value, 'group', perm)  12 us
    all_to_all x1, waiting for transfers between devices, on_device(): losses = lax.all_to_all(part, 'dp', 0, 0)  8.09 us
    ppermute x8, waiting for transfers between devices, shift_x(): return lax.ppermute(value, ('group', 'dp'), perm)  6.4 us
    pallas_call x1, Pallas kernels, grads(): pl.pallas_call(grad_kernel, out_shape=jax.ShapeDtypeStruct((B, E), jnp.fl...  6.05 us
  transfers between devices with their start and end apart: 12, of which 4 were waited for; matrix products, arithmetic and copies ran while one was open for 0% of the time, Pallas kernels for 17%

profile of v4, /device:TPU:1, one launch (start us, length us, event | category | flops | bytes accessed | tf_op | source)
XLA Modules:
  0.0 98.3 jit_solution(4310424210034657344)
XLA Ops:
  0.6 0.0 copy-start
  0.6 1.0 %copy-done = f32[256,512]{1,0:T(8,128)S(1)} copy-done((f32[256,512]{1,0:T(8,128)S(1)}, f32[256,512]{1,0:T(8,128)}, u32[]{:S(2)}) %copy-start) | copy-done | bytes 524312
  1.7 0.1 shard_map.41.first_ref
  1.8 4.4 %collective-permute-start.4 = (bf16[256,512]{1,0:T(8,128)(2,1)S(1)}, bf16[256,512]{1,0:T(8,128)(2,1)S(1)}, u32[]{:S(2)}, u32[]{:S(2)}) collective-permute-start(bf16[256,512]{1,0:T(8,128)(2,1)S(1)} %shard_map.41.first_ref), channel_id=1, source_target_pairs={{0,32},{32,0},{64,96},{96,64},{128,160},{160,128},{192,224},{224,1... | collective-permute-start | bytes 786440 | tf_op jit(solution)/shard_map/ppermute | solution.py:268
  6.2 4.9 %collective-permute-start = (bf16[256,512]{1,0:T(8,128)(2,1)S(1)}, bf16[256,512]{1,0:T(8,128)(2,1)S(1)}, u32[]{:S(2)}, u32[]{:S(2)}) collective-permute-start(bf16[256,512]{1,0:T(8,128)(2,1)S(1)} %shard_map.41.first_ref), channel_id=1, source_target_pairs={{0,64},{32,96},{64,0},{96,32},{128,192},{160,224},{192,128},{224,1... | collective-permute-start | bytes 786440 | tf_op jit(solution)/shard_map/ppermute | solution.py:268
  11.1 1.2 %shard_map.43 = (s32[16,256]{1,0:T(8,128)S(1)}, s32[256,128]{1,0:T(8,128)S(1)}) custom-call(s32[1024,128]{1,0:T(8,128)} %bitcast.1), custom_call_target="tpu_custom_call" | custom-call | tf_op jit(solution)/shard_map/pallas_call | solution.py:94
  12.3 0.0 collective-permute-done.4.second_ref
  12.4 3.1 %collective-permute-start.6 = (bf16[512,512]{1,0:T(8,128)(2,1)S(1)}, bf16[512,512]{1,0:T(8,128)(2,1)S(1)}, u32[]{:S(2)}, u32[]{:S(2)}) collective-permute-start(bf16[512,512]{1,0:T(8,128)(2,1)S(1)} %shard_map.44.refs_0_), channel_id=1, source_target_pairs={{0,384},{1,129},{2,386},{3,131},{4,388},{5,133},{6,390},{7,135},{8... | collective-permute-start | bytes 1572872 | tf_op jit(solution)/shard_map/ppermute | solution.py:263
  15.5 3.4 %collective-permute-start.5 = (bf16[512,512]{1,0:T(8,128)(2,1)S(1)}, bf16[512,512]{1,0:T(8,128)(2,1)S(1)}, u32[]{:S(2)}, u32[]{:S(2)}) collective-permute-start(bf16[512,512]{1,0:T(8,128)(2,1)S(1)} %shard_map.44.refs_0_), channel_id=1, source_target_pairs={{0,128},{1,385},{2,130},{3,387},{4,132},{5,389},{6,134},{7,391},{8... | collective-permute-start | bytes 1572872 | tf_op jit(solution)/shard_map/ppermute | solution.py:263
  18.9 0.0 collective-permute-done.refs_1_
  18.9 2.7 %collective-permute-start.2 = (bf16[256,512]{1,0:T(8,128)(2,1)S(1)}, bf16[256,512]{1,0:T(8,128)(2,1)S(1)}, u32[]{:S(2)}, u32[]{:S(2)}) collective-permute-start(bf16[256,512]{1,0:T(8,128)(2,1)S(1)} %collective-permute-done.refs_1_), channel_id=1, source_target_pairs={{0,32},{32,0},{64,96},{96,64},{128,160},{160,128},{192,224},{224,1... | collective-permute-start | bytes 786440 | tf_op jit(solution)/shard_map/ppermute | solution.py:268
  21.7 7.2 %collective-permute-start.7 = (bf16[256,512]{1,0:T(8,128)(2,1)S(1)}, bf16[256,512]{1,0:T(8,128)(2,1)S(1)}, u32[]{:S(2)}, u32[]{:S(2)}) collective-permute-start(bf16[256,512]{1,0:T(8,128)(2,1)S(1)} %collective-permute-done.refs_1_), channel_id=1, source_target_pairs={{0,128},{1,385},{2,130},{3,387},{4,132},{5,389},{6,134},{7,391},{8... | collective-permute-start | bytes 786440 | tf_op jit(solution)/shard_map/ppermute | solution.py:263
  28.8 1.9 %collective-permute-start.1 = (bf16[256,512]{1,0:T(8,128)(2,1)S(1)}, bf16[256,512]{1,0:T(8,128)(2,1)S(1)}, u32[]{:S(2)}, u32[]{:S(2)}) collective-permute-start(bf16[256,512]{1,0:T(8,128)(2,1)S(1)} %collective-permute-done.refs_1_), channel_id=1, source_target_pairs={{0,384},{1,129},{2,386},{3,131},{4,388},{5,133},{6,390},{7,135},{8... | collective-permute-start | bytes 786440 | tf_op jit(solution)/shard_map/ppermute | solution.py:263
  30.8 0.0 collective-permute-done.2.refs_2_
  30.8 3.0 %collective-permute-start.3 = (bf16[256,512]{1,0:T(8,128)(2,1)S(1)}, bf16[256,512]{1,0:T(8,128)(2,1)S(1)}, u32[]{:S(2)}, u32[]{:S(2)}) collective-permute-start(bf16[256,512]{1,0:T(8,128)(2,1)S(1)} %collective-permute-done.2.refs_2_), channel_id=1, source_target_pairs={{0,384},{1,129},{2,386},{3,131},{4,388},{5,133},{6,390},{7,135},{8... | collective-permute-start | bytes 786440 | tf_op jit(solution)/shard_map/ppermute | solution.py:263
  33.8 0.4 collective-permute-done.7.refs_5_
  34.2 4.3 %collective-permute-start.8 = (bf16[256,512]{1,0:T(8,128)(2,1)S(1)}, bf16[256,512]{1,0:T(8,128)(2,1)S(1)}, u32[]{:S(2)}, u32[]{:S(2)}) collective-permute-start(bf16[256,512]{1,0:T(8,128)(2,1)S(1)} %collective-permute-done.2.refs_2_), channel_id=1, source_target_pairs={{0,128},{1,385},{2,130},{3,387},{4,132},{5,389},{6,134},{7,391},{8... | collective-permute-start | bytes 786440 | tf_op jit(solution)/shard_map/ppermute | solution.py:263
  38.5 0.0 collective-permute-done.6.refs_4_
  38.5 0.0 collective-permute-done.5.refs_3_
  38.5 2.3 %collective-permute-start.9 = (bf16[512,512]{1,0:T(8,128)(2,1)S(1)}, bf16[512,512]{1,0:T(8,128)(2,1)S(1)}, u32[]{:S(2)}, u32[]{:S(2)}) collective-permute-start(bf16[512,512]{1,0:T(8,128)(2,1)S(1)} %collective-permute-done.5.refs_3_), channel_id=1, source_target_pairs={{0,128},{1,385},{2,130},{3,387},{4,132},{5,389},{6,134},{7,391},{8... | collective-permute-start | bytes 1572872 | tf_op jit(solution)/shard_map/ppermute | solution.py:263
  40.7 0.0 collective-permute-done.1.first_ref.refs_7_
  40.8 1.0 collective-permute-done.3.second_ref.refs_8_
  41.8 2.1 %collective-permute-start.10 = (bf16[512,512]{1,0:T(8,128)(2,1)S(1)}, bf16[512,512]{1,0:T(8,128)(2,1)S(1)}, u32[]{:S(2)}, u32[]{:S(2)}) collective-permute-start(bf16[512,512]{1,0:T(8,128)(2,1)S(1)} %shard_map.42), channel_id=1, source_target_pairs={{0,384},{1,129},{2,386},{3,131},{4,388},{5,133},{6,390},{7,135},{8... | collective-permute-start | bytes 1572872 | tf_op jit(solution)/shard_map/ppermute | solution.py:263
  43.8 3.8 %shard_map.45 = (f32[24,256]{1,0:T(8,128)S(1)}, bf16[2048,512]{1,0:T(8,128)(2,1)}) custom-call(bf16[512,512]{1,0:T(8,128)(2,1)S(1)} %shard_map.44.refs_0_, bf16[256,512]{1,0:T(8,128)(2,1)S(1)} %collective-permute-done.refs_1_, bf16[256,512]{1,0:T(8,128)(2,1)S(1)} %collective-permute-done.2.refs_2_, bf16[512,512]{1,0:T(8,128)(2,1)S(1)} %collective-permute-done.5.refs_3_, ...), custom_call_target="tpu_custom_call" | custom-call | flops 2415919104 | bytes 2097152 | tf_op jit(solution)/shard_map/pallas_call | solution.py:177
  47.7 0.0 collective-permute-done.8.refs_6_
  47.7 3.7 %shard_map.46 = (f32[24,256]{1,0:T(8,128)S(1)}, bf16[1024,512]{1,0:T(8,128)(2,1)}) custom-call(bf16[512,512]{1,0:T(8,128)(2,1)S(1)} %shard_map.44.refs_0_, bf16[256,512]{1,0:T(8,128)(2,1)S(1)} %collective-permute-done.refs_1_, bf16[256,512]{1,0:T(8,128)(2,1)S(1)} %collective-permute-done.2.refs_2_, bf16[512,512]{1,0:T(8,128)(2,1)S(1)} %collective-permute-done.5.refs_3_, ...), custom_call_target="tpu_custom_call" | custom-call | flops 2818572288 | bytes 3145728 | tf_op jit(solution)/shard_map/pallas_call | solution.py:177
  51.4 0.0 collective-permute-done.9.refs_9_
  51.4 2.3 %shard_map.47 = (f32[24,256]{1,0:T(8,128)S(1)}, bf16[512,512]{1,0:T(8,128)(2,1)}) custom-call(bf16[512,512]{1,0:T(8,128)(2,1)S(1)} %shard_map.44.refs_0_, bf16[256,512]{1,0:T(8,128)(2,1)S(1)} %collective-permute-done.refs_1_, bf16[256,512]{1,0:T(8,128)(2,1)S(1)} %collective-permute-done.2.refs_2_, bf16[512,512]{1,0:T(8,128)(2,1)S(1)} %collective-permute-done.5.refs_3_, ...), custom_call_target="tpu_custom_call" | custom-call | flops 1811939328 | bytes 3670016 | tf_op jit(solution)/shard_map/pallas_call | solution.py:177
  53.7 5.1 %collective-permute-done.10.refs_10_ = bf16[512,512]{1,0:T(8,128)(2,1)S(1)} collective-permute-done((bf16[512,512]{1,0:T(8,128)(2,1)S(1)}, bf16[512,512]{1,0:T(8,128)(2,1)S(1)}, u32[]{:S(2)}, u32[]{:S(2)}) %collective-permute-start.10) | collective-permute-done | bytes 524320 | tf_op jit(solution)/shard_map/ppermute | solution.py:263
  58.8 0.0 copy-start.1
  58.8 3.4 %shard_map.48 = (f32[24,256]{1,0:T(8,128)S(1)}, bf16[512,512]{1,0:T(8,128)(2,1)}, f32[32,1,128]{2,1,0:T(1,128)}) custom-call(bf16[512,512]{1,0:T(8,128)(2,1)S(1)} %shard_map.44.refs_0_, bf16[256,512]{1,0:T(8,128)(2,1)S(1)} %collective-permute-done.refs_1_, bf16[256,512]{1,0:T(8,128)(2,1)S(1)} %collective-permute-done.2.refs_2_, ...), custom_call_target="tpu_custom_call" | custom-call | flops 2080374784 | bytes 4194304 | tf_op jit(solution)/shard_map/pallas_call | solution.py:177
  62.2 19.6 %all-to-all-start = ((f32[32,1,128]{2,1,0:T(1,128)}), f32[32,1,128]{2,1,0:T(1,128)S(1)}, u32[]{:S(2)}, u32[]{:S(2)}) async-start(f32[32,1,128]{2,1,0:T(1,128)} %get-tuple-element.39), calls=%async_computation | async-start | bytes 32768 | tf_op jit(solution)/shard_map/all_to_all | solution.py:318
  81.8 0.0 copy-done.1
  81.8 6.0 %shard_map.49 = f32[256,512]{1,0:T(8,128)} custom-call(bf16[2048,512]{1,0:T(8,128)(2,1)} %get-tuple-element.28.refs_0_, bf16[1024,512]{1,0:T(8,128)(2,1)} %get-tuple-element.31.refs_1_, bf16[512,512]{1,0:T(8,128)(2,1)} %get-tuple-element.33.refs_2_, bf16[512,512]{1,0:T(8,128)(2,1)} %get-tuple-element.36.refs_3_, s32[256,128]{1,0:T(8,128)S(1)} %get-tuple-element.37.refs_4_, ...), custom_call_target="tpu_custom_call" | custom-call | flops 3221225472 | bytes 4194304 | tf_op jit(solution)/shard_map/pallas_call | solution.py:239
  87.8 8.1 %all-to-all-done = f32[32,1,128]{2,1,0:T(1,128)S(1)} async-done(((f32[32,1,128]{2,1,0:T(1,128)}), f32[32,1,128]{2,1,0:T(1,128)S(1)}, u32[]{:S(2)}, u32[]{:S(2)}) %all-to-all-start) | async-done | bytes 16416 | tf_op jit(solution)/shard_map/all_to_all | solution.py:318
  95.9 0.6 reduce_sum.9
  (2 shorter events, 0.1 us)
Async XLA Ops:
  0.6 1.0 %copy-start = (f32[256,512]{1,0:T(8,128)S(1)}, f32[256,512]{1,0:T(8,128)}, u32[]{:S(2)}) copy-start(f32[256,512]{1,0:T(8,128)} %refs_6_.1) | copy-start | bytes 1572868
  1.8 10.5 %collective-permute-start.4 = (bf16[256,512]{1,0:T(8,128)(2,1)S(1)}, bf16[256,512]{1,0:T(8,128)(2,1)S(1)}, u32[]{:S(2)}, u32[]{:S(2)}) collective-permute-start(bf16[256,512]{1,0:T(8,128)(2,1)S(1)} %shard_map.41.first_ref), channel_id=1, source_target_pairs={{0,32},{32,0},{64,96},{96,64},{128,160},{160,128},{192,224},{224,1... | collective-permute-start | bytes 786440 | tf_op jit(solution)/shard_map/ppermute | solution.py:268
  6.2 12.7 %collective-permute-start = (bf16[256,512]{1,0:T(8,128)(2,1)S(1)}, bf16[256,512]{1,0:T(8,128)(2,1)S(1)}, u32[]{:S(2)}, u32[]{:S(2)}) collective-permute-start(bf16[256,512]{1,0:T(8,128)(2,1)S(1)} %shard_map.41.first_ref), channel_id=1, source_target_pairs={{0,64},{32,96},{64,0},{96,32},{128,192},{160,224},{192,128},{224,1... | collective-permute-start | bytes 786440 | tf_op jit(solution)/shard_map/ppermute | solution.py:268
  12.4 26.1 %collective-permute-start.6 = (bf16[512,512]{1,0:T(8,128)(2,1)S(1)}, bf16[512,512]{1,0:T(8,128)(2,1)S(1)}, u32[]{:S(2)}, u32[]{:S(2)}) collective-permute-start(bf16[512,512]{1,0:T(8,128)(2,1)S(1)} %shard_map.44.refs_0_), channel_id=1, source_target_pairs={{0,384},{1,129},{2,386},{3,131},{4,388},{5,133},{6,390},{7,135},{8... | collective-permute-start | bytes 1572872 | tf_op jit(solution)/shard_map/ppermute | solution.py:263
  15.5 22.9 %collective-permute-start.5 = (bf16[512,512]{1,0:T(8,128)(2,1)S(1)}, bf16[512,512]{1,0:T(8,128)(2,1)S(1)}, u32[]{:S(2)}, u32[]{:S(2)}) collective-permute-start(bf16[512,512]{1,0:T(8,128)(2,1)S(1)} %shard_map.44.refs_0_), channel_id=1, source_target_pairs={{0,128},{1,385},{2,130},{3,387},{4,132},{5,389},{6,134},{7,391},{8... | collective-permute-start | bytes 1572872 | tf_op jit(solution)/shard_map/ppermute | solution.py:263
  18.9 11.8 %collective-permute-start.2 = (bf16[256,512]{1,0:T(8,128)(2,1)S(1)}, bf16[256,512]{1,0:T(8,128)(2,1)S(1)}, u32[]{:S(2)}, u32[]{:S(2)}) collective-permute-start(bf16[256,512]{1,0:T(8,128)(2,1)S(1)} %collective-permute-done.refs_1_), channel_id=1, source_target_pairs={{0,32},{32,0},{64,96},{96,64},{128,160},{160,128},{192,224},{224,1... | collective-permute-start | bytes 786440 | tf_op jit(solution)/shard_map/ppermute | solution.py:268
  21.7 12.5 %collective-permute-start.7 = (bf16[256,512]{1,0:T(8,128)(2,1)S(1)}, bf16[256,512]{1,0:T(8,128)(2,1)S(1)}, u32[]{:S(2)}, u32[]{:S(2)}) collective-permute-start(bf16[256,512]{1,0:T(8,128)(2,1)S(1)} %collective-permute-done.refs_1_), channel_id=1, source_target_pairs={{0,128},{1,385},{2,130},{3,387},{4,132},{5,389},{6,134},{7,391},{8... | collective-permute-start | bytes 786440 | tf_op jit(solution)/shard_map/ppermute | solution.py:263
  28.8 11.9 %collective-permute-start.1 = (bf16[256,512]{1,0:T(8,128)(2,1)S(1)}, bf16[256,512]{1,0:T(8,128)(2,1)S(1)}, u32[]{:S(2)}, u32[]{:S(2)}) collective-permute-start(bf16[256,512]{1,0:T(8,128)(2,1)S(1)} %collective-permute-done.refs_1_), channel_id=1, source_target_pairs={{0,384},{1,129},{2,386},{3,131},{4,388},{5,133},{6,390},{7,135},{8... | collective-permute-start | bytes 786440 | tf_op jit(solution)/shard_map/ppermute | solution.py:263
  30.8 10.9 %collective-permute-start.3 = (bf16[256,512]{1,0:T(8,128)(2,1)S(1)}, bf16[256,512]{1,0:T(8,128)(2,1)S(1)}, u32[]{:S(2)}, u32[]{:S(2)}) collective-permute-start(bf16[256,512]{1,0:T(8,128)(2,1)S(1)} %collective-permute-done.2.refs_2_), channel_id=1, source_target_pairs={{0,384},{1,129},{2,386},{3,131},{4,388},{5,133},{6,390},{7,135},{8... | collective-permute-start | bytes 786440 | tf_op jit(solution)/shard_map/ppermute | solution.py:263
  34.2 13.5 %collective-permute-start.8 = (bf16[256,512]{1,0:T(8,128)(2,1)S(1)}, bf16[256,512]{1,0:T(8,128)(2,1)S(1)}, u32[]{:S(2)}, u32[]{:S(2)}) collective-permute-start(bf16[256,512]{1,0:T(8,128)(2,1)S(1)} %collective-permute-done.2.refs_2_), channel_id=1, source_target_pairs={{0,128},{1,385},{2,130},{3,387},{4,132},{5,389},{6,134},{7,391},{8... | collective-permute-start | bytes 786440 | tf_op jit(solution)/shard_map/ppermute | solution.py:263
  38.5 12.9 %collective-permute-start.9 = (bf16[512,512]{1,0:T(8,128)(2,1)S(1)}, bf16[512,512]{1,0:T(8,128)(2,1)S(1)}, u32[]{:S(2)}, u32[]{:S(2)}) collective-permute-start(bf16[512,512]{1,0:T(8,128)(2,1)S(1)} %collective-permute-done.5.refs_3_), channel_id=1, source_target_pairs={{0,128},{1,385},{2,130},{3,387},{4,132},{5,389},{6,134},{7,391},{8... | collective-permute-start | bytes 1572872 | tf_op jit(solution)/shard_map/ppermute | solution.py:263
  41.8 17.0 %collective-permute-start.10 = (bf16[512,512]{1,0:T(8,128)(2,1)S(1)}, bf16[512,512]{1,0:T(8,128)(2,1)S(1)}, u32[]{:S(2)}, u32[]{:S(2)}) collective-permute-start(bf16[512,512]{1,0:T(8,128)(2,1)S(1)} %shard_map.42), channel_id=1, source_target_pairs={{0,384},{1,129},{2,386},{3,131},{4,388},{5,133},{6,390},{7,135},{8... | collective-permute-start | bytes 1572872 | tf_op jit(solution)/shard_map/ppermute | solution.py:263
  58.8 23.0 %copy-start.1 = (f32[256,512]{1,0:T(8,128)S(1)}, f32[256,512]{1,0:T(8,128)}, u32[]{:S(2)}) copy-start(f32[256,512]{1,0:T(8,128)} %refs_6_.1) | copy-start | bytes 1572868
  62.2 33.7 %all-to-all-start = ((f32[32,1,128]{2,1,0:T(1,128)}), f32[32,1,128]{2,1,0:T(1,128)S(1)}, u32[]{:S(2)}, u32[]{:S(2)}) async-start(f32[32,1,128]{2,1,0:T(1,128)} %get-tuple-element.39), calls=%async_computation | async-start | bytes 32768 | tf_op jit(solution)/shard_map/all_to_all | solution.py:318

commit v5 on v3

--- a/solution.py
+++ b/solution.py
@@ -263,6 +263,15 @@
     return lax.ppermute(value, ("group", "dp"), perm)
 
 
+def loss_groups(dp_count):
+    segments = ((3, 3, 0, 0), (0, 0, 3, 3), (1, 1, 2, 2), (2, 2, 1, 1))
+    return [
+        [(x * Z + lows[k // 2 % 4]) * dp_count + k for k in range(dp_count)]
+        for x in range(X)
+        for lows in segments
+    ]
+
+
 def swap_z(value, mask):
     perm = [(x * Z + z, x * Z + (z ^ mask)) for x in range(X) for z in range(Z)]
     return lax.ppermute(value, "group", perm)
@@ -316,7 +325,7 @@
     state, _ = add(z2_1, z3_1, z2_3, z3_3)
     state, _ = add(near_2)
     (totals,), (part,) = add(far_2)
-    losses = lax.all_to_all(part, "dp", 0, 0)
+    losses = lax.all_to_all(part, ("group", "dp"), 0, 0, axis_index_groups=loss_groups(dp_count))
     gradient = grads(units, own_place, totals, embeddings)
     loss = jnp.sum(losses) / (B * dp_count * group_count)
     return (gradient, loss)

time: 98 us -> 96.3 us (0.983)
  the two profiles are of different devices: /device:TPU:1 before, /device:TPU:33 now
where the time goes in v5:
time: 96.3 us; the launch traced here: 95.8 us
  starting transfers between devices  59 us (61%)
  Pallas kernels  20.6 us (21%)
  waiting for transfers between devices  11.9 us (12%)
  between operations  2.66 us (3%)
  local copies, waits for them, and re-layouts  1.04 us (1%)
    ppermute x8, starting transfers between devices, shift_x(): return lax.ppermute(value, ('group', 'dp'), perm)  30.4 us
    all_to_all x1, starting transfers between devices, on_device(): lax.all_to_all(part, ('group', 'dp'), 0, 0, axis_index_groups=loss_groups...  19.7 us
    pallas_call x5, Pallas kernels, sums(): pl.pallas_call(functools.partial(sums_kernel, first, last, len(old) + len...  13.1 us
    ppermute x3, starting transfers between devices, swap_z(): return lax.ppermute(value, 'group', perm)  8.95 us
    all_to_all x1, waiting for transfers between devices, on_device(): lax.all_to_all(part, ('group', 'dp'), 0, 0, axis_index_groups=loss_groups...  7.18 us
    pallas_call x1, Pallas kernels, grads(): pl.pallas_call(grad_kernel, out_shape=jax.ShapeDtypeStruct((B, E), jnp.fl...  6.06 us
    ppermute x8, waiting for transfers between devices, shift_x(): return lax.ppermute(value, ('group', 'dp'), perm)  4.4 us
  transfers between devices with their start and end apart: 12, of which 3 were waited for; matrix products, arithmetic and copies ran while one was open for 0% of the time, Pallas kernels for 18%

profile of v5, /device:TPU:33, one launch (start us, length us, event | category | flops | bytes accessed | tf_op | source)
XLA Modules:
  0.0 95.8 jit_solution(4406769220183155211)
XLA Ops:
  0.6 0.0 copy-start
  0.6 1.0 %copy-done = f32[256,512]{1,0:T(8,128)S(1)} copy-done((f32[256,512]{1,0:T(8,128)S(1)}, f32[256,512]{1,0:T(8,128)}, u32[]{:S(2)}) %copy-start) | copy-done | bytes 524312
  1.7 0.1 shard_map.41.first_ref
  1.8 1.9 %collective-permute-start.4 = (bf16[256,512]{1,0:T(8,128)(2,1)S(1)}, bf16[256,512]{1,0:T(8,128)(2,1)S(1)}, u32[]{:S(2)}, u32[]{:S(2)}) collective-permute-start(bf16[256,512]{1,0:T(8,128)(2,1)S(1)} %shard_map.41.first_ref), channel_id=1, source_target_pairs={{0,32},{32,0},{64,96},{96,64},{128,160},{160,128},{192,224},{224,1... | collective-permute-start | bytes 786440 | tf_op jit(solution)/shard_map/ppermute | solution.py:277
  3.8 4.9 %collective-permute-start = (bf16[256,512]{1,0:T(8,128)(2,1)S(1)}, bf16[256,512]{1,0:T(8,128)(2,1)S(1)}, u32[]{:S(2)}, u32[]{:S(2)}) collective-permute-start(bf16[256,512]{1,0:T(8,128)(2,1)S(1)} %shard_map.41.first_ref), channel_id=1, source_target_pairs={{0,64},{32,96},{64,0},{96,32},{128,192},{160,224},{192,128},{224,1... | collective-permute-start | bytes 786440 | tf_op jit(solution)/shard_map/ppermute | solution.py:277
  8.7 0.3 collective-permute-done.4.second_ref
  9.0 5.1 %collective-permute-start.6 = (bf16[512,512]{1,0:T(8,128)(2,1)S(1)}, bf16[512,512]{1,0:T(8,128)(2,1)S(1)}, u32[]{:S(2)}, u32[]{:S(2)}) collective-permute-start(bf16[512,512]{1,0:T(8,128)(2,1)S(1)} %shard_map.44.refs_0_), channel_id=1, source_target_pairs={{0,384},{1,129},{2,386},{3,131},{4,388},{5,133},{6,390},{7,135},{8... | collective-permute-start | bytes 1572872 | tf_op jit(solution)/shard_map/ppermute | solution.py:263
  14.1 3.2 %collective-permute-start.5 = (bf16[512,512]{1,0:T(8,128)(2,1)S(1)}, bf16[512,512]{1,0:T(8,128)(2,1)S(1)}, u32[]{:S(2)}, u32[]{:S(2)}) collective-permute-start(bf16[512,512]{1,0:T(8,128)(2,1)S(1)} %shard_map.44.refs_0_), channel_id=1, source_target_pairs={{0,128},{1,385},{2,130},{3,387},{4,132},{5,389},{6,134},{7,391},{8... | collective-permute-start | bytes 1572872 | tf_op jit(solution)/shard_map/ppermute | solution.py:263
  17.3 0.0 collective-permute-done.refs_1_
  17.3 2.1 %collective-permute-start.2 = (bf16[256,512]{1,0:T(8,128)(2,1)S(1)}, bf16[256,512]{1,0:T(8,128)(2,1)S(1)}, u32[]{:S(2)}, u32[]{:S(2)}) collective-permute-start(bf16[256,512]{1,0:T(8,128)(2,1)S(1)} %collective-permute-done.refs_1_), channel_id=1, source_target_pairs={{0,32},{32,0},{64,96},{96,64},{128,160},{160,128},{192,224},{224,1... | collective-permute-start | bytes 786440 | tf_op jit(solution)/shard_map/ppermute | solution.py:277
  19.4 8.4 %collective-permute-start.7 = (bf16[256,512]{1,0:T(8,128)(2,1)S(1)}, bf16[256,512]{1,0:T(8,128)(2,1)S(1)}, u32[]{:S(2)}, u32[]{:S(2)}) collective-permute-start(bf16[256,512]{1,0:T(8,128)(2,1)S(1)} %collective-permute-done.refs_1_), channel_id=1, source_target_pairs={{0,128},{1,385},{2,130},{3,387},{4,132},{5,389},{6,134},{7,391},{8... | collective-permute-start | bytes 786440 | tf_op jit(solution)/shard_map/ppermute | solution.py:263
  27.8 1.2 %shard_map.42 = (s32[16,256]{1,0:T(8,128)S(1)}, s32[256,128]{1,0:T(8,128)S(1)}) custom-call(s32[1024,128]{1,0:T(8,128)} %bitcast.1), custom_call_target="tpu_custom_call" | custom-call | tf_op jit(solution)/shard_map/pallas_call | solution.py:94
  29.0 1.9 %collective-permute-start.1 = (bf16[256,512]{1,0:T(8,128)(2,1)S(1)}, bf16[256,512]{1,0:T(8,128)(2,1)S(1)}, u32[]{:S(2)}, u32[]{:S(2)}) collective-permute-start(bf16[256,512]{1,0:T(8,128)(2,1)S(1)} %collective-permute-done.refs_1_), channel_id=1, source_target_pairs={{0,384},{1,129},{2,386},{3,131},{4,388},{5,133},{6,390},{7,135},{8... | collective-permute-start | bytes 786440 | tf_op jit(solution)/shard_map/ppermute | solution.py:263
  31.0 0.0 collective-permute-done.2.refs_2_
  31.0 2.1 %collective-permute-start.3 = (bf16[256,512]{1,0:T(8,128)(2,1)S(1)}, bf16[256,512]{1,0:T(8,128)(2,1)S(1)}, u32[]{:S(2)}, u32[]{:S(2)}) collective-permute-start(bf16[256,512]{1,0:T(8,128)(2,1)S(1)} %collective-permute-done.2.refs_2_), channel_id=1, source_target_pairs={{0,384},{1,129},{2,386},{3,131},{4,388},{5,133},{6,390},{7,135},{8... | collective-permute-start | bytes 786440 | tf_op jit(solution)/shard_map/ppermute | solution.py:263
  33.1 0.0 collective-permute-done.7.refs_5_
  33.1 4.4 %collective-permute-start.8 = (bf16[256,512]{1,0:T(8,128)(2,1)S(1)}, bf16[256,512]{1,0:T(8,128)(2,1)S(1)}, u32[]{:S(2)}, u32[]{:S(2)}) collective-permute-start(bf16[256,512]{1,0:T(8,128)(2,1)S(1)} %collective-permute-done.2.refs_2_), channel_id=1, source_target_pairs={{0,128},{1,385},{2,130},{3,387},{4,132},{5,389},{6,134},{7,391},{8... | collective-permute-start | bytes 786440 | tf_op jit(solution)/shard_map/ppermute | solution.py:263
  37.5 0.0 collective-permute-done.6.refs_4_
  37.5 0.0 collective-permute-done.5.refs_3_
  37.5 3.4 %collective-permute-start.9 = (bf16[512,512]{1,0:T(8,128)(2,1)S(1)}, bf16[512,512]{1,0:T(8,128)(2,1)S(1)}, u32[]{:S(2)}, u32[]{:S(2)}) collective-permute-start(bf16[512,512]{1,0:T(8,128)(2,1)S(1)} %collective-permute-done.5.refs_3_), channel_id=1, source_target_pairs={{0,128},{1,385},{2,130},{3,387},{4,132},{5,389},{6,134},{7,391},{8... | collective-permute-start | bytes 1572872 | tf_op jit(solution)/shard_map/ppermute | solution.py:263
  40.9 0.0 collective-permute-done.1.first_ref.refs_7_
  40.9 0.0 collective-permute-done.3.second_ref.refs_8_
  41.0 1.9 %collective-permute-start.10 = (bf16[512,512]{1,0:T(8,128)(2,1)S(1)}, bf16[512,512]{1,0:T(8,128)(2,1)S(1)}, u32[]{:S(2)}, u32[]{:S(2)}) collective-permute-start(bf16[512,512]{1,0:T(8,128)(2,1)S(1)} %shard_map.43), channel_id=1, source_target_pairs={{0,384},{1,129},{2,386},{3,131},{4,388},{5,133},{6,390},{7,135},{8... | collective-permute-start | bytes 1572872 | tf_op jit(solution)/shard_map/ppermute | solution.py:263
  42.9 1.4 %shard_map.45 = (f32[24,256]{1,0:T(8,128)S(1)}, bf16[1024,512]{1,0:T(8,128)(2,1)}) custom-call(bf16[512,512]{1,0:T(8,128)(2,1)S(1)} %shard_map.44.refs_0_, bf16[256,512]{1,0:T(8,128)(2,1)S(1)} %collective-permute-done.refs_1_, bf16[256,512]{1,0:T(8,128)(2,1)S(1)} %collective-permute-done.2.refs_2_, ...), custom_call_target="tpu_custom_call" | custom-call | flops 671088640 | bytes 1048576 | tf_op jit(solution)/shard_map/pallas_call | solution.py:177
  44.3 2.5 %shard_map.46 = (f32[24,256]{1,0:T(8,128)S(1)}, bf16[1024,512]{1,0:T(8,128)(2,1)}) custom-call(bf16[512,512]{1,0:T(8,128)(2,1)S(1)} %shard_map.44.refs_0_, bf16[256,512]{1,0:T(8,128)(2,1)S(1)} %collective-permute-done.refs_1_, bf16[256,512]{1,0:T(8,128)(2,1)S(1)} %collective-permute-done.2.refs_2_, bf16[512,512]{1,0:T(8,128)(2,1)S(1)} %collective-permute-done.5.refs_3_, ...), custom_call_target="tpu_custom_call" | custom-call | flops 1744830464 | bytes 2097152 | tf_op jit(solution)/shard_map/pallas_call | solution.py:177
  46.8 0.0 collective-permute-done.8.refs_6_
  46.8 3.7 %shard_map.47 = (f32[24,256]{1,0:T(8,128)S(1)}, bf16[1024,512]{1,0:T(8,128)(2,1)}) custom-call(bf16[512,512]{1,0:T(8,128)(2,1)S(1)} %shard_map.44.refs_0_, bf16[256,512]{1,0:T(8,128)(2,1)S(1)} %collective-permute-done.refs_1_, bf16[256,512]{1,0:T(8,128)(2,1)S(1)} %collective-permute-done.2.refs_2_, bf16[512,512]{1,0:T(8,128)(2,1)S(1)} %collective-permute-done.5.refs_3_, ...), custom_call_target="tpu_custom_call" | custom-call | flops 2818572288 | bytes 3145728 | tf_op jit(solution)/shard_map/pallas_call | solution.py:177
  50.5 0.0 collective-permute-done.9.refs_9_
  50.5 2.3 %shard_map.48 = (f32[24,256]{1,0:T(8,128)S(1)}, bf16[512,512]{1,0:T(8,128)(2,1)}) custom-call(bf16[512,512]{1,0:T(8,128)(2,1)S(1)} %shard_map.44.refs_0_, bf16[256,512]{1,0:T(8,128)(2,1)S(1)} %collective-permute-done.refs_1_, bf16[256,512]{1,0:T(8,128)(2,1)S(1)} %collective-permute-done.2.refs_2_, bf16[512,512]{1,0:T(8,128)(2,1)S(1)} %collective-permute-done.5.refs_3_, ...), custom_call_target="tpu_custom_call" | custom-call | flops 1811939328 | bytes 3670016 | tf_op jit(solution)/shard_map/pallas_call | solution.py:177
  52.9 4.4 %collective-permute-done.10.refs_10_ = bf16[512,512]{1,0:T(8,128)(2,1)S(1)} collective-permute-done((bf16[512,512]{1,0:T(8,128)(2,1)S(1)}, bf16[512,512]{1,0:T(8,128)(2,1)S(1)}, u32[]{:S(2)}, u32[]{:S(2)}) %collective-permute-start.10) | collective-permute-done | bytes 524320 | tf_op jit(solution)/shard_map/ppermute | solution.py:263
  57.2 0.0 copy-start.1
  57.2 3.2 %shard_map.49 = (f32[24,256]{1,0:T(8,128)S(1)}, bf16[512,512]{1,0:T(8,128)(2,1)}, f32[32,1,128]{2,1,0:T(1,128)}) custom-call(bf16[512,512]{1,0:T(8,128)(2,1)S(1)} %shard_map.44.refs_0_, bf16[256,512]{1,0:T(8,128)(2,1)S(1)} %collective-permute-done.refs_1_, bf16[256,512]{1,0:T(8,128)(2,1)S(1)} %collective-permute-done.2.refs_2_, ...), custom_call_target="tpu_custom_call" | custom-call | flops 2080374784 | bytes 4194304 | tf_op jit(solution)/shard_map/pallas_call | solution.py:177
  60.4 19.7 %all-to-all-start = ((f32[32,1,128]{2,1,0:T(1,128)}), f32[32,1,128]{2,1,0:T(1,128)S(1)}, u32[]{:S(2)}, u32[]{:S(2)}) async-start(f32[32,1,128]{2,1,0:T(1,128)} %get-tuple-element.43), calls=%async_computation | async-start | bytes 32768 | tf_op jit(solution)/shard_map/all_to_all | solution.py:328
  80.1 0.0 copy-done.1
  80.1 6.1 %shard_map.50 = f32[256,512]{1,0:T(8,128)} custom-call(bf16[1024,512]{1,0:T(8,128)(2,1)} %get-tuple-element.28.refs_0_, bf16[1024,512]{1,0:T(8,128)(2,1)} %get-tuple-element.32.refs_1_, bf16[1024,512]{1,0:T(8,128)(2,1)} %get-tuple-element.35.refs_2_, bf16[512,512]{1,0:T(8,128)(2,1)} %get-tuple-element.37.refs_3_, ...), custom_call_target="tpu_custom_call" | custom-call | flops 3221225472 | bytes 4194304 | tf_op jit(solution)/shard_map/pallas_call | solution.py:239
  86.2 7.2 %all-to-all-done = f32[32,1,128]{2,1,0:T(1,128)S(1)} async-done(((f32[32,1,128]{2,1,0:T(1,128)}), f32[32,1,128]{2,1,0:T(1,128)S(1)}, u32[]{:S(2)}, u32[]{:S(2)}) %all-to-all-start) | async-done | bytes 16416 | tf_op jit(solution)/shard_map/all_to_all | solution.py:328
  93.4 0.6 reduce_sum.9
  (2 shorter events, 0.1 us)
Async XLA Ops:
  0.6 1.0 %copy-start = (f32[256,512]{1,0:T(8,128)S(1)}, f32[256,512]{1,0:T(8,128)}, u32[]{:S(2)}) copy-start(f32[256,512]{1,0:T(8,128)} %refs_7_.1) | copy-start | bytes 1572868
  1.8 7.1 %collective-permute-start.4 = (bf16[256,512]{1,0:T(8,128)(2,1)S(1)}, bf16[256,512]{1,0:T(8,128)(2,1)S(1)}, u32[]{:S(2)}, u32[]{:S(2)}) collective-permute-start(bf16[256,512]{1,0:T(8,128)(2,1)S(1)} %shard_map.41.first_ref), channel_id=1, source_target_pairs={{0,32},{32,0},{64,96},{96,64},{128,160},{160,128},{192,224},{224,1... | collective-permute-start | bytes 786440 | tf_op jit(solution)/shard_map/ppermute | solution.py:277
  3.8 13.5 %collective-permute-start = (bf16[256,512]{1,0:T(8,128)(2,1)S(1)}, bf16[256,512]{1,0:T(8,128)(2,1)S(1)}, u32[]{:S(2)}, u32[]{:S(2)}) collective-permute-start(bf16[256,512]{1,0:T(8,128)(2,1)S(1)} %shard_map.41.first_ref), channel_id=1, source_target_pairs={{0,64},{32,96},{64,0},{96,32},{128,192},{160,224},{192,128},{224,1... | collective-permute-start | bytes 786440 | tf_op jit(solution)/shard_map/ppermute | solution.py:277
  9.0 28.5 %collective-permute-start.6 = (bf16[512,512]{1,0:T(8,128)(2,1)S(1)}, bf16[512,512]{1,0:T(8,128)(2,1)S(1)}, u32[]{:S(2)}, u32[]{:S(2)}) collective-permute-start(bf16[512,512]{1,0:T(8,128)(2,1)S(1)} %shard_map.44.refs_0_), channel_id=1, source_target_pairs={{0,384},{1,129},{2,386},{3,131},{4,388},{5,133},{6,390},{7,135},{8... | collective-permute-start | bytes 1572872 | tf_op jit(solution)/shard_map/ppermute | solution.py:263
  14.1 23.5 %collective-permute-start.5 = (bf16[512,512]{1,0:T(8,128)(2,1)S(1)}, bf16[512,512]{1,0:T(8,128)(2,1)S(1)}, u32[]{:S(2)}, u32[]{:S(2)}) collective-permute-start(bf16[512,512]{1,0:T(8,128)(2,1)S(1)} %shard_map.44.refs_0_), channel_id=1, source_target_pairs={{0,128},{1,385},{2,130},{3,387},{4,132},{5,389},{6,134},{7,391},{8... | collective-permute-start | bytes 1572872 | tf_op jit(solution)/shard_map/ppermute | solution.py:263
  17.3 13.7 %collective-permute-start.2 = (bf16[256,512]{1,0:T(8,128)(2,1)S(1)}, bf16[256,512]{1,0:T(8,128)(2,1)S(1)}, u32[]{:S(2)}, u32[]{:S(2)}) collective-permute-start(bf16[256,512]{1,0:T(8,128)(2,1)S(1)} %collective-permute-done.refs_1_), channel_id=1, source_target_pairs={{0,32},{32,0},{64,96},{96,64},{128,160},{160,128},{192,224},{224,1... | collective-permute-start | bytes 786440 | tf_op jit(solution)/shard_map/ppermute | solution.py:277
  19.4 13.7 %collective-permute-start.7 = (bf16[256,512]{1,0:T(8,128)(2,1)S(1)}, bf16[256,512]{1,0:T(8,128)(2,1)S(1)}, u32[]{:S(2)}, u32[]{:S(2)}) collective-permute-start(bf16[256,512]{1,0:T(8,128)(2,1)S(1)} %collective-permute-done.refs_1_), channel_id=1, source_target_pairs={{0,128},{1,385},{2,130},{3,387},{4,132},{5,389},{6,134},{7,391},{8... | collective-permute-start | bytes 786440 | tf_op jit(solution)/shard_map/ppermute | solution.py:263
  29.0 11.9 %collective-permute-start.1 = (bf16[256,512]{1,0:T(8,128)(2,1)S(1)}, bf16[256,512]{1,0:T(8,128)(2,1)S(1)}, u32[]{:S(2)}, u32[]{:S(2)}) collective-permute-start(bf16[256,512]{1,0:T(8,128)(2,1)S(1)} %collective-permute-done.refs_1_), channel_id=1, source_target_pairs={{0,384},{1,129},{2,386},{3,131},{4,388},{5,133},{6,390},{7,135},{8... | collective-permute-start | bytes 786440 | tf_op jit(solution)/shard_map/ppermute | solution.py:263
  31.0 9.9 %collective-permute-start.3 = (bf16[256,512]{1,0:T(8,128)(2,1)S(1)}, bf16[256,512]{1,0:T(8,128)(2,1)S(1)}, u32[]{:S(2)}, u32[]{:S(2)}) collective-permute-start(bf16[256,512]{1,0:T(8,128)(2,1)S(1)} %collective-permute-done.2.refs_2_), channel_id=1, source_target_pairs={{0,384},{1,129},{2,386},{3,131},{4,388},{5,133},{6,390},{7,135},{8... | collective-permute-start | bytes 786440 | tf_op jit(solution)/shard_map/ppermute | solution.py:263
  33.1 13.7 %collective-permute-start.8 = (bf16[256,512]{1,0:T(8,128)(2,1)S(1)}, bf16[256,512]{1,0:T(8,128)(2,1)S(1)}, u32[]{:S(2)}, u32[]{:S(2)}) collective-permute-start(bf16[256,512]{1,0:T(8,128)(2,1)S(1)} %collective-permute-done.2.refs_2_), channel_id=1, source_target_pairs={{0,128},{1,385},{2,130},{3,387},{4,132},{5,389},{6,134},{7,391},{8... | collective-permute-start | bytes 786440 | tf_op jit(solution)/shard_map/ppermute | solution.py:263
  37.5 13.0 %collective-permute-start.9 = (bf16[512,512]{1,0:T(8,128)(2,1)S(1)}, bf16[512,512]{1,0:T(8,128)(2,1)S(1)}, u32[]{:S(2)}, u32[]{:S(2)}) collective-permute-start(bf16[512,512]{1,0:T(8,128)(2,1)S(1)} %collective-permute-done.5.refs_3_), channel_id=1, source_target_pairs={{0,128},{1,385},{2,130},{3,387},{4,132},{5,389},{6,134},{7,391},{8... | collective-permute-start | bytes 1572872 | tf_op jit(solution)/shard_map/ppermute | solution.py:263
  41.0 16.3 %collective-permute-start.10 = (bf16[512,512]{1,0:T(8,128)(2,1)S(1)}, bf16[512,512]{1,0:T(8,128)(2,1)S(1)}, u32[]{:S(2)}, u32[]{:S(2)}) collective-permute-start(bf16[512,512]{1,0:T(8,128)(2,1)S(1)} %shard_map.43), channel_id=1, source_target_pairs={{0,384},{1,129},{2,386},{3,131},{4,388},{5,133},{6,390},{7,135},{8... | collective-permute-start | bytes 1572872 | tf_op jit(solution)/shard_map/ppermute | solution.py:263
  57.2 22.9 %copy-start.1 = (f32[256,512]{1,0:T(8,128)S(1)}, f32[256,512]{1,0:T(8,128)}, u32[]{:S(2)}) copy-start(f32[256,512]{1,0:T(8,128)} %refs_7_.1) | copy-start | bytes 1572868
  60.4 32.9 %all-to-all-start = ((f32[32,1,128]{2,1,0:T(1,128)}), f32[32,1,128]{2,1,0:T(1,128)S(1)}, u32[]{:S(2)}, u32[]{:S(2)}) async-start(f32[32,1,128]{2,1,0:T(1,128)} %get-tuple-element.43), calls=%async_computation | async-start | bytes 32768 | tf_op jit(solution)/shard_map/all_to_all | solution.py:328

commit v6 on v5

--- a/solution.py
+++ b/solution.py
@@ -302,7 +302,7 @@
     z2 = swap_z(packed, 2)
     near = stack(packed, z1)
     near_1, near_3 = shift_x(near, 1), shift_x(near, 3)
-    z3, place, own_place = lax.optimization_barrier((swap_z(z2, 1), place, own_place))
+    z3 = swap_z(z2, 1)
     z2_1, z2_3 = shift_x(z2, 1), shift_x(z2, 3)
     z3_1, z3_3 = shift_x(z3, 1), shift_x(z3, 3)
 

time: 96.3 us -> 94.5 us (0.981)
  the two profiles are of different devices: /device:TPU:33 before, /device:TPU:1 now
where the time goes in v6:
time: 94.5 us; the launch traced here: 93.7 us
  starting transfers between devices  59.2 us (63%)
  Pallas kernels  20.6 us (22%)
  waiting for transfers between devices  9.48 us (10%)
  between operations  2.67 us (3%)
  local copies, waits for them, and re-layouts  1.04 us (1%)
    ppermute x8, starting transfers between devices, shift_x(): return lax.ppermute(value, ('group', 'dp'), perm)  28.8 us
    all_to_all x1, starting transfers between devices, on_device(): lax.all_to_all(part, ('group', 'dp'), 0, 0, axis_index_groups=loss_groups...  18 us
    pallas_call x5, Pallas kernels, sums(): pl.pallas_call(functools.partial(sums_kernel, first, last, len(old) + len...  13.1 us
    ppermute x3, starting transfers between devices, swap_z(): return lax.ppermute(value, 'group', perm)  12.4 us
    pallas_call x1, Pallas kernels, grads(): pl.pallas_call(grad_kernel, out_shape=jax.ShapeDtypeStruct((B, E), jnp.fl...  6.06 us
    all_to_all x1, waiting for transfers between devices, on_device(): lax.all_to_all(part, ('group', 'dp'), 0, 0, axis_index_groups=loss_groups...  5.39 us
    ppermute x8, waiting for transfers between devices, shift_x(): return lax.ppermute(value, ('group', 'dp'), perm)  4.09 us
  transfers between devices with their start and end apart: 12, of which 3 were waited for; matrix products, arithmetic and copies ran while one was open for 0% of the time, Pallas kernels for 18%

profile of v6, /device:TPU:1, one launch (start us, length us, event | category | flops | bytes accessed | tf_op | source)
XLA Modules:
  0.0 93.7 jit_solution(13525266350100365084)
XLA Ops:
  0.6 0.0 copy-start
  0.6 1.0 %copy-done = f32[256,512]{1,0:T(8,128)S(1)} copy-done((f32[256,512]{1,0:T(8,128)S(1)}, f32[256,512]{1,0:T(8,128)}, u32[]{:S(2)}) %copy-start) | copy-done | bytes 524312
  1.7 0.1 shard_map.41.first_ref
  1.8 4.4 %collective-permute-start.4 = (bf16[256,512]{1,0:T(8,128)(2,1)S(1)}, bf16[256,512]{1,0:T(8,128)(2,1)S(1)}, u32[]{:S(2)}, u32[]{:S(2)}) collective-permute-start(bf16[256,512]{1,0:T(8,128)(2,1)S(1)} %shard_map.41.first_ref), channel_id=1, source_target_pairs={{0,32},{32,0},{64,96},{96,64},{128,160},{160,128},{192,224},{224,1... | collective-permute-start | bytes 786440 | tf_op jit(solution)/shard_map/ppermute | solution.py:277
  6.2 4.9 %collective-permute-start = (bf16[256,512]{1,0:T(8,128)(2,1)S(1)}, bf16[256,512]{1,0:T(8,128)(2,1)S(1)}, u32[]{:S(2)}, u32[]{:S(2)}) collective-permute-start(bf16[256,512]{1,0:T(8,128)(2,1)S(1)} %shard_map.41.first_ref), channel_id=1, source_target_pairs={{0,64},{32,96},{64,0},{96,32},{128,192},{160,224},{192,128},{224,1... | collective-permute-start | bytes 786440 | tf_op jit(solution)/shard_map/ppermute | solution.py:277
  11.1 0.0 collective-permute-done.4.second_ref
  11.2 4.1 %collective-permute-start.6 = (bf16[512,512]{1,0:T(8,128)(2,1)S(1)}, bf16[512,512]{1,0:T(8,128)(2,1)S(1)}, u32[]{:S(2)}, u32[]{:S(2)}) collective-permute-start(bf16[512,512]{1,0:T(8,128)(2,1)S(1)} %shard_map.43.refs_0_), channel_id=1, source_target_pairs={{0,384},{1,129},{2,386},{3,131},{4,388},{5,133},{6,390},{7,135},{8... | collective-permute-start | bytes 1572872 | tf_op jit(solution)/shard_map/ppermute | solution.py:263
  15.3 3.2 %collective-permute-start.5 = (bf16[512,512]{1,0:T(8,128)(2,1)S(1)}, bf16[512,512]{1,0:T(8,128)(2,1)S(1)}, u32[]{:S(2)}, u32[]{:S(2)}) collective-permute-start(bf16[512,512]{1,0:T(8,128)(2,1)S(1)} %shard_map.43.refs_0_), channel_id=1, source_target_pairs={{0,128},{1,385},{2,130},{3,387},{4,132},{5,389},{6,134},{7,391},{8... | collective-permute-start | bytes 1572872 | tf_op jit(solution)/shard_map/ppermute | solution.py:263
  18.5 0.0 collective-permute-done.refs_1_
  18.5 3.2 %collective-permute-start.2 = (bf16[256,512]{1,0:T(8,128)(2,1)S(1)}, bf16[256,512]{1,0:T(8,128)(2,1)S(1)}, u32[]{:S(2)}, u32[]{:S(2)}) collective-permute-start(bf16[256,512]{1,0:T(8,128)(2,1)S(1)} %collective-permute-done.refs_1_), channel_id=1, source_target_pairs={{0,32},{32,0},{64,96},{96,64},{128,160},{160,128},{192,224},{224,1... | collective-permute-start | bytes 786440 | tf_op jit(solution)/shard_map/ppermute | solution.py:277
  21.7 7.2 %collective-permute-start.7 = (bf16[256,512]{1,0:T(8,128)(2,1)S(1)}, bf16[256,512]{1,0:T(8,128)(2,1)S(1)}, u32[]{:S(2)}, u32[]{:S(2)}) collective-permute-start(bf16[256,512]{1,0:T(8,128)(2,1)S(1)} %collective-permute-done.refs_1_), channel_id=1, source_target_pairs={{0,128},{1,385},{2,130},{3,387},{4,132},{5,389},{6,134},{7,391},{8... | collective-permute-start | bytes 786440 | tf_op jit(solution)/shard_map/ppermute | solution.py:263
  28.8 1.9 %collective-permute-start.1 = (bf16[256,512]{1,0:T(8,128)(2,1)S(1)}, bf16[256,512]{1,0:T(8,128)(2,1)S(1)}, u32[]{:S(2)}, u32[]{:S(2)}) collective-permute-start(bf16[256,512]{1,0:T(8,128)(2,1)S(1)} %collective-permute-done.refs_1_), channel_id=1, source_target_pairs={{0,384},{1,129},{2,386},{3,131},{4,388},{5,133},{6,390},{7,135},{8... | collective-permute-start | bytes 786440 | tf_op jit(solution)/shard_map/ppermute | solution.py:263
  30.8 0.0 collective-permute-done.2.refs_2_
  30.8 3.0 %collective-permute-start.3 = (bf16[256,512]{1,0:T(8,128)(2,1)S(1)}, bf16[256,512]{1,0:T(8,128)(2,1)S(1)}, u32[]{:S(2)}, u32[]{:S(2)}) collective-permute-start(bf16[256,512]{1,0:T(8,128)(2,1)S(1)} %collective-permute-done.2.refs_2_), channel_id=1, source_target_pairs={{0,384},{1,129},{2,386},{3,131},{4,388},{5,133},{6,390},{7,135},{8... | collective-permute-start | bytes 786440 | tf_op jit(solution)/shard_map/ppermute | solution.py:263
  33.8 0.1 collective-permute-done.7.refs_5_
  33.9 4.1 %collective-permute-start.8 = (bf16[256,512]{1,0:T(8,128)(2,1)S(1)}, bf16[256,512]{1,0:T(8,128)(2,1)S(1)}, u32[]{:S(2)}, u32[]{:S(2)}) collective-permute-start(bf16[256,512]{1,0:T(8,128)(2,1)S(1)} %collective-permute-done.2.refs_2_), channel_id=1, source_target_pairs={{0,128},{1,385},{2,130},{3,387},{4,132},{5,389},{6,134},{7,391},{8... | collective-permute-start | bytes 786440 | tf_op jit(solution)/shard_map/ppermute | solution.py:263
  38.0 0.0 collective-permute-done.6.refs_4_
  38.0 0.0 collective-permute-done.5.refs_3_
  38.1 2.6 %collective-permute-start.9 = (bf16[512,512]{1,0:T(8,128)(2,1)S(1)}, bf16[512,512]{1,0:T(8,128)(2,1)S(1)}, u32[]{:S(2)}, u32[]{:S(2)}) collective-permute-start(bf16[512,512]{1,0:T(8,128)(2,1)S(1)} %collective-permute-done.5.refs_3_), channel_id=1, source_target_pairs={{0,128},{1,385},{2,130},{3,387},{4,132},{5,389},{6,134},{7,391},{8... | collective-permute-start | bytes 1572872 | tf_op jit(solution)/shard_map/ppermute | solution.py:263
  40.7 1.2 %shard_map.44 = (s32[16,256]{1,0:T(8,128)S(1)}, s32[256,128]{1,0:T(8,128)S(1)}) custom-call(s32[1024,128]{1,0:T(8,128)} %bitcast.1), custom_call_target="tpu_custom_call" | custom-call | tf_op jit(solution)/shard_map/pallas_call | solution.py:94
  41.9 0.0 collective-permute-done.1.first_ref.refs_7_
  41.9 0.0 collective-permute-done.3.second_ref.refs_8_
  42.0 2.7 %collective-permute-start.10 = (bf16[512,512]{1,0:T(8,128)(2,1)S(1)}, bf16[512,512]{1,0:T(8,128)(2,1)S(1)}, u32[]{:S(2)}, u32[]{:S(2)}) collective-permute-start(bf16[512,512]{1,0:T(8,128)(2,1)S(1)} %shard_map.42), channel_id=1, source_target_pairs={{0,384},{1,129},{2,386},{3,131},{4,388},{5,133},{6,390},{7,135},{8... | collective-permute-start | bytes 1572872 | tf_op jit(solution)/shard_map/ppermute | solution.py:263
  44.6 1.4 %shard_map.45 = (f32[24,256]{1,0:T(8,128)S(1)}, bf16[1024,512]{1,0:T(8,128)(2,1)}) custom-call(bf16[512,512]{1,0:T(8,128)(2,1)S(1)} %shard_map.43.refs_0_, bf16[256,512]{1,0:T(8,128)(2,1)S(1)} %collective-permute-done.refs_1_, bf16[256,512]{1,0:T(8,128)(2,1)S(1)} %collective-permute-done.2.refs_2_, ...), custom_call_target="tpu_custom_call" | custom-call | flops 671088640 | bytes 1048576 | tf_op jit(solution)/shard_map/pallas_call | solution.py:177
  46.1 2.5 %shard_map.46 = (f32[24,256]{1,0:T(8,128)S(1)}, bf16[1024,512]{1,0:T(8,128)(2,1)}) custom-call(bf16[512,512]{1,0:T(8,128)(2,1)S(1)} %shard_map.43.refs_0_, bf16[256,512]{1,0:T(8,128)(2,1)S(1)} %collective-permute-done.refs_1_, bf16[256,512]{1,0:T(8,128)(2,1)S(1)} %collective-permute-done.2.refs_2_, bf16[512,512]{1,0:T(8,128)(2,1)S(1)} %collective-permute-done.5.refs_3_, ...), custom_call_target="tpu_custom_call" | custom-call | flops 1744830464 | bytes 2097152 | tf_op jit(solution)/shard_map/pallas_call | solution.py:177
  48.6 0.0 collective-permute-done.8.refs_6_
  48.6 3.7 %shard_map.47 = (f32[24,256]{1,0:T(8,128)S(1)}, bf16[1024,512]{1,0:T(8,128)(2,1)}) custom-call(bf16[512,512]{1,0:T(8,128)(2,1)S(1)} %shard_map.43.refs_0_, bf16[256,512]{1,0:T(8,128)(2,1)S(1)} %collective-permute-done.refs_1_, bf16[256,512]{1,0:T(8,128)(2,1)S(1)} %collective-permute-done.2.refs_2_, bf16[512,512]{1,0:T(8,128)(2,1)S(1)} %collective-permute-done.5.refs_3_, ...), custom_call_target="tpu_custom_call" | custom-call | flops 2818572288 | bytes 3145728 | tf_op jit(solution)/shard_map/pallas_call | solution.py:177
  52.3 0.0 collective-permute-done.9.refs_9_
  52.3 2.3 %shard_map.48 = (f32[24,256]{1,0:T(8,128)S(1)}, bf16[512,512]{1,0:T(8,128)(2,1)}) custom-call(bf16[512,512]{1,0:T(8,128)(2,1)S(1)} %shard_map.43.refs_0_, bf16[256,512]{1,0:T(8,128)(2,1)S(1)} %collective-permute-done.refs_1_, bf16[256,512]{1,0:T(8,128)(2,1)S(1)} %collective-permute-done.2.refs_2_, bf16[512,512]{1,0:T(8,128)(2,1)S(1)} %collective-permute-done.5.refs_3_, ...), custom_call_target="tpu_custom_call" | custom-call | flops 1811939328 | bytes 3670016 | tf_op jit(solution)/shard_map/pallas_call | solution.py:177
  54.6 4.0 %collective-permute-done.10.refs_10_ = bf16[512,512]{1,0:T(8,128)(2,1)S(1)} collective-permute-done((bf16[512,512]{1,0:T(8,128)(2,1)S(1)}, bf16[512,512]{1,0:T(8,128)(2,1)S(1)}, u32[]{:S(2)}, u32[]{:S(2)}) %collective-permute-start.10) | collective-permute-done | bytes 524320 | tf_op jit(solution)/shard_map/ppermute | solution.py:263
  58.6 0.0 copy-start.1
  58.6 3.2 %shard_map.49 = (f32[24,256]{1,0:T(8,128)S(1)}, bf16[512,512]{1,0:T(8,128)(2,1)}, f32[32,1,128]{2,1,0:T(1,128)}) custom-call(bf16[512,512]{1,0:T(8,128)(2,1)S(1)} %shard_map.43.refs_0_, bf16[256,512]{1,0:T(8,128)(2,1)S(1)} %collective-permute-done.refs_1_, bf16[256,512]{1,0:T(8,128)(2,1)S(1)} %collective-permute-done.2.refs_2_, ...), custom_call_target="tpu_custom_call" | custom-call | flops 2080374784 | bytes 4194304 | tf_op jit(solution)/shard_map/pallas_call | solution.py:177
  61.8 18.0 %all-to-all-start = ((f32[32,1,128]{2,1,0:T(1,128)}), f32[32,1,128]{2,1,0:T(1,128)S(1)}, u32[]{:S(2)}, u32[]{:S(2)}) async-start(f32[32,1,128]{2,1,0:T(1,128)} %get-tuple-element.37), calls=%async_computation | async-start | bytes 32768 | tf_op jit(solution)/shard_map/all_to_all | solution.py:328
  79.8 0.0 copy-done.1
  79.8 6.1 %shard_map.50 = f32[256,512]{1,0:T(8,128)} custom-call(bf16[1024,512]{1,0:T(8,128)(2,1)} %get-tuple-element.22.refs_0_, bf16[1024,512]{1,0:T(8,128)(2,1)} %get-tuple-element.26.refs_1_, bf16[1024,512]{1,0:T(8,128)(2,1)} %get-tuple-element.29.refs_2_, bf16[512,512]{1,0:T(8,128)(2,1)} %get-tuple-element.31.refs_3_, ...), custom_call_target="tpu_custom_call" | custom-call | flops 3221225472 | bytes 4194304 | tf_op jit(solution)/shard_map/pallas_call | solution.py:239
  85.9 5.4 %all-to-all-done = f32[32,1,128]{2,1,0:T(1,128)S(1)} async-done(((f32[32,1,128]{2,1,0:T(1,128)}), f32[32,1,128]{2,1,0:T(1,128)S(1)}, u32[]{:S(2)}, u32[]{:S(2)}) %all-to-all-start) | async-done | bytes 16416 | tf_op jit(solution)/shard_map/all_to_all | solution.py:328
  91.3 0.6 reduce_sum.9
  (2 shorter events, 0.1 us)
Async XLA Ops:
  0.6 1.0 %copy-start = (f32[256,512]{1,0:T(8,128)S(1)}, f32[256,512]{1,0:T(8,128)}, u32[]{:S(2)}) copy-start(f32[256,512]{1,0:T(8,128)} %refs_7_.1) | copy-start | bytes 1572868
  1.8 9.3 %collective-permute-start.4 = (bf16[256,512]{1,0:T(8,128)(2,1)S(1)}, bf16[256,512]{1,0:T(8,128)(2,1)S(1)}, u32[]{:S(2)}, u32[]{:S(2)}) collective-permute-start(bf16[256,512]{1,0:T(8,128)(2,1)S(1)} %shard_map.41.first_ref), channel_id=1, source_target_pairs={{0,32},{32,0},{64,96},{96,64},{128,160},{160,128},{192,224},{224,1... | collective-permute-start | bytes 786440 | tf_op jit(solution)/shard_map/ppermute | solution.py:277
  6.2 12.3 %collective-permute-start = (bf16[256,512]{1,0:T(8,128)(2,1)S(1)}, bf16[256,512]{1,0:T(8,128)(2,1)S(1)}, u32[]{:S(2)}, u32[]{:S(2)}) collective-permute-start(bf16[256,512]{1,0:T(8,128)(2,1)S(1)} %shard_map.41.first_ref), channel_id=1, source_target_pairs={{0,64},{32,96},{64,0},{96,32},{128,192},{160,224},{192,128},{224,1... | collective-permute-start | bytes 786440 | tf_op jit(solution)/shard_map/ppermute | solution.py:277
  11.2 26.9 %collective-permute-start.6 = (bf16[512,512]{1,0:T(8,128)(2,1)S(1)}, bf16[512,512]{1,0:T(8,128)(2,1)S(1)}, u32[]{:S(2)}, u32[]{:S(2)}) collective-permute-start(bf16[512,512]{1,0:T(8,128)(2,1)S(1)} %shard_map.43.refs_0_), channel_id=1, source_target_pairs={{0,384},{1,129},{2,386},{3,131},{4,388},{5,133},{6,390},{7,135},{8... | collective-permute-start | bytes 1572872 | tf_op jit(solution)/shard_map/ppermute | solution.py:263
  15.3 22.8 %collective-permute-start.5 = (bf16[512,512]{1,0:T(8,128)(2,1)S(1)}, bf16[512,512]{1,0:T(8,128)(2,1)S(1)}, u32[]{:S(2)}, u32[]{:S(2)}) collective-permute-start(bf16[512,512]{1,0:T(8,128)(2,1)S(1)} %shard_map.43.refs_0_), channel_id=1, source_target_pairs={{0,128},{1,385},{2,130},{3,387},{4,132},{5,389},{6,134},{7,391},{8... | collective-permute-start | bytes 1572872 | tf_op jit(solution)/shard_map/ppermute | solution.py:263
  18.5 12.3 %collective-permute-start.2 = (bf16[256,512]{1,0:T(8,128)(2,1)S(1)}, bf16[256,512]{1,0:T(8,128)(2,1)S(1)}, u32[]{:S(2)}, u32[]{:S(2)}) collective-permute-start(bf16[256,512]{1,0:T(8,128)(2,1)S(1)} %collective-permute-done.refs_1_), channel_id=1, source_target_pairs={{0,32},{32,0},{64,96},{96,64},{128,160},{160,128},{192,224},{224,1... | collective-permute-start | bytes 786440 | tf_op jit(solution)/shard_map/ppermute | solution.py:277
  21.7 12.3 %collective-permute-start.7 = (bf16[256,512]{1,0:T(8,128)(2,1)S(1)}, bf16[256,512]{1,0:T(8,128)(2,1)S(1)}, u32[]{:S(2)}, u32[]{:S(2)}) collective-permute-start(bf16[256,512]{1,0:T(8,128)(2,1)S(1)} %collective-permute-done.refs_1_), channel_id=1, source_target_pairs={{0,128},{1,385},{2,130},{3,387},{4,132},{5,389},{6,134},{7,391},{8... | collective-permute-start | bytes 786440 | tf_op jit(solution)/shard_map/ppermute | solution.py:263
  28.8 13.1 %collective-permute-start.1 = (bf16[256,512]{1,0:T(8,128)(2,1)S(1)}, bf16[256,512]{1,0:T(8,128)(2,1)S(1)}, u32[]{:S(2)}, u32[]{:S(2)}) collective-permute-start(bf16[256,512]{1,0:T(8,128)(2,1)S(1)} %collective-permute-done.refs_1_), channel_id=1, source_target_pairs={{0,384},{1,129},{2,386},{3,131},{4,388},{5,133},{6,390},{7,135},{8... | collective-permute-start | bytes 786440 | tf_op jit(solution)/shard_map/ppermute | solution.py:263
  30.8 11.1 %collective-permute-start.3 = (bf16[256,512]{1,0:T(8,128)(2,1)S(1)}, bf16[256,512]{1,0:T(8,128)(2,1)S(1)}, u32[]{:S(2)}, u32[]{:S(2)}) collective-permute-start(bf16[256,512]{1,0:T(8,128)(2,1)S(1)} %collective-permute-done.2.refs_2_), channel_id=1, source_target_pairs={{0,384},{1,129},{2,386},{3,131},{4,388},{5,133},{6,390},{7,135},{8... | collective-permute-start | bytes 786440 | tf_op jit(solution)/shard_map/ppermute | solution.py:263
  33.9 14.7 %collective-permute-start.8 = (bf16[256,512]{1,0:T(8,128)(2,1)S(1)}, bf16[256,512]{1,0:T(8,128)(2,1)S(1)}, u32[]{:S(2)}, u32[]{:S(2)}) collective-permute-start(bf16[256,512]{1,0:T(8,128)(2,1)S(1)} %collective-permute-done.2.refs_2_), channel_id=1, source_target_pairs={{0,128},{1,385},{2,130},{3,387},{4,132},{5,389},{6,134},{7,391},{8... | collective-permute-start | bytes 786440 | tf_op jit(solution)/shard_map/ppermute | solution.py:263
  38.1 14.2 %collective-permute-start.9 = (bf16[512,512]{1,0:T(8,128)(2,1)S(1)}, bf16[512,512]{1,0:T(8,128)(2,1)S(1)}, u32[]{:S(2)}, u32[]{:S(2)}) collective-permute-start(bf16[512,512]{1,0:T(8,128)(2,1)S(1)} %collective-permute-done.5.refs_3_), channel_id=1, source_target_pairs={{0,128},{1,385},{2,130},{3,387},{4,132},{5,389},{6,134},{7,391},{8... | collective-permute-start | bytes 1572872 | tf_op jit(solution)/shard_map/ppermute | solution.py:263
  42.0 16.6 %collective-permute-start.10 = (bf16[512,512]{1,0:T(8,128)(2,1)S(1)}, bf16[512,512]{1,0:T(8,128)(2,1)S(1)}, u32[]{:S(2)}, u32[]{:S(2)}) collective-permute-start(bf16[512,512]{1,0:T(8,128)(2,1)S(1)} %shard_map.42), channel_id=1, source_target_pairs={{0,384},{1,129},{2,386},{3,131},{4,388},{5,133},{6,390},{7,135},{8... | collective-permute-start | bytes 1572872 | tf_op jit(solution)/shard_map/ppermute | solution.py:263
  58.6 21.2 %copy-start.1 = (f32[256,512]{1,0:T(8,128)S(1)}, f32[256,512]{1,0:T(8,128)}, u32[]{:S(2)}) copy-start(f32[256,512]{1,0:T(8,128)} %refs_7_.1) | copy-start | bytes 1572868
  61.8 29.5 %all-to-all-start = ((f32[32,1,128]{2,1,0:T(1,128)}), f32[32,1,128]{2,1,0:T(1,128)S(1)}, u32[]{:S(2)}, u32[]{:S(2)}) async-start(f32[32,1,128]{2,1,0:T(1,128)} %get-tuple-element.37), calls=%async_computation | async-start | bytes 32768 | tf_op jit(solution)/shard_map/all_to_all | solution.py:328
